TPU v7x, 32 devices: a whole 2x2x4 slice. The times are simulated.
32 devices in a mesh: ra: 8 (over y, x, core), dec: 4 (over z).
Axes of the slice: x: 2, y: 2, z: 4, core: 2. Of those that a mesh axis runs over, the one named last changes fastest.
Arguments:
- log_flux: float32 [5, 8192], P(None, ('ra', 'dec')), may hold values from 5.5 to 9.5
- position: float32 [2, 8192], P(None, ('ra', 'dec')), may hold values from 0 to 640
- log_width: float32 [8192], P(('ra', 'dec')), may hold values from -3.5 to -0.5
- owner_tile: int32 [8192, 1], P(('ra', 'dec')), may hold values from 0 to 31; in each aligned block of 256 rows (0 to 255, 256 to 511, ...) at most 16 rows name the same one
- sky_level: float32 [8, 4, 5], P('ra', 'dec'), may hold values from 0.5 to 4
- counts: int32 [5, 5120, 2560], P(None, 'ra', 'dec'), may hold values from 0 to 7
Outputs:
- gradient: float32 [8, 8192], P(None, ('ra', 'dec'))
Inputs may be any that keep to these rules, and one draw needn't show every extreme that they name: `owner_tile`: in each aligned block of 256 catalog rows (the rows of one device) no tile is named more than 16 times, a bound that some block reaches.
All inputs are finite; a program needn't handle non-finite values.
Results may differ from a plain program's by a relative error of at most 0.00095.
Values may be sent and summed in bfloat16 or wider, within the bound.
No kernel may reach another device: no remote copies, remote signals or barrier semaphores. Data moves between devices by JAX's collectives and lax.ppermute only.
A program may use at most 128 MiB of HBM per device.

v0:
```python
import math

import jax
import jax.numpy as jnp
from jax import lax
from jax.sharding import PartitionSpec as P

MARGIN = 128
CAT_DEV = 256


def passed_along(value, axis, steps):
    count = lax.axis_size(axis)
    leading, last = (max(0, -steps), min(count, count - steps))
    return lax.ppermute(value, axis, [(source, source + steps) for source in range(leading, last)])


def with_halo(cells, sides, width):
    for axis, dim in sides:
        count = lax.axis_size(axis)
        ends = count - 1
        head = lax.slice_in_dim(cells, 0, width, axis=dim)
        tail = lax.slice_in_dim(cells, cells.shape[dim] - width, cells.shape[dim], axis=dim)
        cells = jnp.concatenate(
            [
                lax.ppermute(tail, axis, [(i, (i + 1) % count) for i in range(ends)]),
                cells,
                lax.ppermute(head, axis, [((i + 1) % count, i) for i in range(ends)]),
            ],
            axis=dim,
        )
    return cells


def profiles(center, log_width, length):
    coords = jnp.arange(length, dtype=jnp.float32) - MARGIN + 0.5
    sigma = MARGIN * jnp.exp(log_width)
    offset = (coords[:, None] - center[None, :]) / sigma[None, :]
    shape = jnp.exp(-0.5 * offset * offset) / (math.sqrt(2.0 * math.pi) * sigma[None, :])
    return (shape, offset, sigma)


def on_device(log_flux, position, log_width, owner_tile, sky_level, counts):
    tile_count = lax.axis_size("ra") * lax.axis_size("dec")
    capacity = max(2, 2 * CAT_DEV // tile_count)
    slot_count = tile_count * capacity
    tile_side = counts.shape[1]
    canvas_side = tile_side + 2 * MARGIN
    rows_here = log_flux.shape[1]
    target_tile = owner_tile[:, 0]
    order = jnp.arange(rows_here, dtype=jnp.int32)
    matches = (target_tile[:, None] == target_tile[None, :]) & (order[None, :] < order[:, None])
    rank_in = jnp.sum(matches.astype(jnp.int32), axis=1)
    target_slot = target_tile * capacity + rank_in
    onehot = (target_slot[:, None] == jnp.arange(slot_count, dtype=jnp.int32)[None, :]).astype(
        jnp.float32
    )
    params = jnp.concatenate(
        [log_flux, position, log_width[None, :], jnp.ones((1, rows_here), jnp.float32)], axis=0
    )
    outgoing = jnp.dot(params, onehot, precision=lax.Precision.HIGHEST)
    arrived = lax.all_to_all(outgoing, ("ra", "dec"), split_axis=1, concat_axis=1, tiled=True)
    flux_values = arrived[8][None, :] * jnp.exp(arrived[0:5])
    row_prof, row_off, sigma = profiles(arrived[5], arrived[7], canvas_side)
    col_prof, col_off, _ = profiles(arrived[6], arrived[7], canvas_side)
    row_bf = row_prof.astype(jnp.bfloat16)
    col_bf = col_prof.astype(jnp.bfloat16)
    scaled = (row_prof[None, :, :] * flux_values[:, None, :]).astype(jnp.bfloat16)
    canvas = jnp.einsum("bis,js->bij", scaled, col_bf, preferred_element_type=jnp.float32).astype(
        jnp.bfloat16
    )
    edge = MARGIN
    inner_end = edge + tile_side
    rim_start = tile_side - edge
    interior = canvas[:, edge:inner_end, edge:inner_end].astype(jnp.float32)
    from_below = passed_along(canvas[:, :edge, edge:inner_end], "ra", -1)
    from_above = passed_along(canvas[:, inner_end:, edge:inner_end], "ra", 1)
    from_right = passed_along(canvas[:, edge:inner_end, :edge], "dec", -1)
    from_left = passed_along(canvas[:, edge:inner_end, inner_end:], "dec", 1)
    interior = interior.at[:, rim_start:, :].add(from_below.astype(jnp.float32))
    interior = interior.at[:, :edge, :].add(from_above.astype(jnp.float32))
    interior = interior.at[:, :, rim_start:].add(from_right.astype(jnp.float32))
    interior = interior.at[:, :, :edge].add(from_left.astype(jnp.float32))
    upper_pair = jnp.concatenate([canvas[:, :edge, :edge], canvas[:, :edge, inner_end:]], axis=2)
    lower_pair = jnp.concatenate(
        [canvas[:, inner_end:, :edge], canvas[:, inner_end:, inner_end:]], axis=2
    )
    below_pair = passed_along(upper_pair, "ra", -1)
    above_pair = passed_along(lower_pair, "ra", 1)
    leftward = jnp.concatenate([below_pair[:, :, :edge], above_pair[:, :, :edge]], axis=1)
    rightward = jnp.concatenate([below_pair[:, :, edge:], above_pair[:, :, edge:]], axis=1)
    got_left = passed_along(leftward, "dec", -1).astype(jnp.float32)
    got_right = passed_along(rightward, "dec", 1).astype(jnp.float32)
    interior = interior.at[:, rim_start:, rim_start:].add(got_left[:, :edge])
    interior = interior.at[:, :edge, rim_start:].add(got_left[:, edge:])
    interior = interior.at[:, rim_start:, :edge].add(got_right[:, :edge])
    interior = interior.at[:, :edge, :edge].add(got_right[:, edge:])
    intensity = sky_level.reshape(-1)[:, None, None] + interior
    weights = (counts.astype(jnp.float32) / intensity - 1.0).astype(jnp.bfloat16)
    weight_canvas = with_halo(weights, (("ra", 1), ("dec", 2)), MARGIN)
    along_rows = jnp.einsum(
        "bij,js->bis", weight_canvas, col_bf, preferred_element_type=jnp.float32
    )
    along_cols = jnp.einsum(
        "bij,is->bjs", weight_canvas, row_bf, preferred_element_type=jnp.float32
    )
    flux_grad = flux_values * jnp.sum(row_bf.astype(jnp.float32)[None, :, :] * along_rows, axis=1)
    row_total = jnp.sum(flux_values[:, None, :] * along_rows, axis=0)
    col_total = jnp.sum(flux_values[:, None, :] * along_cols, axis=0)
    row_grad = jnp.sum(row_prof * row_off / sigma[None, :] * row_total, axis=0)
    col_grad = jnp.sum(col_prof * col_off / sigma[None, :] * col_total, axis=0)
    width_grad = jnp.sum(row_prof * (row_off * row_off - 1.0) * row_total, axis=0) + jnp.sum(
        col_prof * (col_off * col_off - 1.0) * col_total, axis=0
    )
    slot_grad = jnp.concatenate(
        [flux_grad, row_grad[None], col_grad[None], width_grad[None]], axis=0
    )
    returned = lax.all_to_all(slot_grad, ("ra", "dec"), split_axis=1, concat_axis=1, tiled=True)
    return jnp.dot(returned, onehot.T, precision=lax.Precision.HIGHEST)


def solution(mesh):
    in_specs = (
        P(None, ("ra", "dec")),
        P(None, ("ra", "dec")),
        P(("ra", "dec")),
        P(("ra", "dec"), None),
        P("ra", "dec", None),
        P(None, "ra", "dec"),
    )
    out_specs = P(None, ("ra", "dec"))
    return jax.shard_map(
        on_device, mesh=mesh, in_specs=in_specs, out_specs=out_specs, check_vma=False
    )
```

profile of v0, /device:TPU:0, one launch (start us, length us, event | category | flops | bytes accessed | tf_op | source)
XLA Modules:
  0.0 196.9 jit_solution(12259774821266721053)
XLA Ops:
  0.0 0.9 convert_reduce_fusion
  0.9 0.7 multiply_add_fusion
  1.7 1.1 fusion.21
  3.0 0.7 reshape.479
  3.7 7.3 %all-to-all-start = ((f32[32,1,144]{2,1,0:T(1,128)}), f32[32,1,144]{2,1,0:T(1,128)S(1)}, u32[]{:S(2)}, u32[]{:S(2)}) async-start(f32[32,1,144]{2,1,0:T(1,128)} %reshape.479), calls=%async_computation | async-start | bytes 65536 | tf_op jit(solution)/shard_map/all_to_all | solution.py:62
  11.0 0.6 fusion.45
  11.7 1.4 and_reduce_fusion
  13.0 10.3 %copy.19 = s32[5,640,640]{1,2,0:T(8,128)} copy(s32[5,640,640]{2,1,0:T(8,128)} %param.27) | data formatting | bytes 16384000 | tf_op args[5]
  23.3 0.5 broadcast.328
  23.8 0.7 reduce.42
  25.5 0.5 fusion.17
  26.0 5.1 %convolution_convert_fusion = bf16[5,896,896]{1,2,0:T(8,128)(2,1)S(1)} fusion(f32[5,512]{1,0:T(8,128)S(1)} %broadcast_multiply_fusion, f32[896,512]{1,0:T(8,128)S(1)} %get-tuple-element.132, f32[512]{0:T(512)S(1)} %mul.154, f32[512]{0:T(512)S(1)} %mul.149, f32[512]{0:T(512)S(1)} %sub.53, f32[896]{0:T(1024)S(1)} %iota_add_fusion), kind=kOutput, calls=%fused_computation.6 | convolution fusion | flops 4121772032 | bytes 9883136 | tf_op jit(solution)/shard_map/bis,js->bij/dot_general | solution.py:69
  31.3 0.3 fusion.41
  31.7 2.2 %collective-permute-start.5 = (bf16[5,128,256]{1,2,0:T(8,128)(2,1)S(1)}, bf16[5,128,256]{1,2,0:T(8,128)(2,1)S(1)}, u32[]{:S(2)}, u32[]{:S(2)}) collective-permute-start(bf16[5,128,256]{1,2,0:T(8,128)(2,1)S(1)} %pad_maximum_fusion.5), channel_id=1, source_target_pairs={{0,4},{4,8},{8,12},{12,16},{16,20},{20,24},{24,28},{1,5},{5,9},{9,... | collective-permute-start | bytes 983048 | tf_op jit(solution)/shard_map/ppermute | solution.py:15
  33.9 1.3 collective-permute-start.4
  35.4 4.2 %collective-permute-start.1 = (bf16[5,128,640]{1,2,0:T(8,128)(2,1)S(1)}, bf16[5,128,640]{1,2,0:T(8,128)(2,1)S(1)}, u32[]{:S(2)}, u32[]{:S(2)}) collective-permute-start(bf16[5,128,640]{1,2,0:T(8,128)(2,1)S(1)} %get-tuple-element.120), channel_id=1, source_target_pairs={{0,4},{4,8},{8,12},{12,16},{16,20},{20,24},{24,28},{1,5},{5,9},{9,... | collective-permute-start | bytes 2457608 | tf_op jit(solution)/shard_map/ppermute | solution.py:15
  39.6 1.3 collective-permute-start
  40.9 1.3 collective-permute-start.2
  42.3 1.3 collective-permute-start.6
  43.7 5.2 %collective-permute-start.7 = (bf16[5,256,128]{1,2,0:T(8,128)(2,1)S(1)}, bf16[5,256,128]{1,2,0:T(8,128)(2,1)S(1)}, u32[]{:S(2)}, u32[]{:S(2)}) collective-permute-start(bf16[5,256,128]{1,2,0:T(8,128)(2,1)S(1)} %pad_maximum_fusion.7), channel_id=1, source_target_pairs={{0,1},{1,2},{2,3},{4,5},{5,6},{6,7},{8,9},{9,10},{10,11},{12,13},{... | collective-permute-start | bytes 983048 | tf_op jit(solution)/shard_map/ppermute | solution.py:15
  48.9 0.6 slice_convert_fusion
  49.4 20.1 %collective-permute-done.6 = bf16[5,256,128]{1,2,0:T(8,128)(2,1)S(1)} collective-permute-done((bf16[5,256,128]{1,2,0:T(8,128)(2,1)S(1)}, bf16[5,256,128]{1,2,0:T(8,128)(2,1)S(1)}, u32[]{:S(2)}, u32[]{:S(2)}) %collective-permute-start.6) | collective-permute-done | bytes 327712 | tf_op jit(solution)/shard_map/ppermute | solution.py:15
  69.5 3.4 %collective-permute-start.3 = (bf16[5,640,128]{1,2,0:T(8,128)(2,1)S(1)}, bf16[5,640,128]{1,2,0:T(8,128)(2,1)S(1)}, u32[]{:S(2)}, u32[]{:S(2)}) collective-permute-start(bf16[5,640,128]{1,2,0:T(8,128)(2,1)S(1)} %get-tuple-element.118), channel_id=1, source_target_pairs={{0,1},{1,2},{2,3},{4,5},{5,6},{6,7},{8,9},{9,10},{10,11},{12,13},{... | collective-permute-start | bytes 2457608 | tf_op jit(solution)/shard_map/ppermute | solution.py:15
  73.4 0.3 fusion.8
  73.8 0.3 fusion.7
  74.1 17.2 %collective-permute-done.3 = bf16[5,640,128]{1,2,0:T(8,128)(2,1)S(1)} collective-permute-done((bf16[5,640,128]{1,2,0:T(8,128)(2,1)S(1)}, bf16[5,640,128]{1,2,0:T(8,128)(2,1)S(1)}, u32[]{:S(2)}, u32[]{:S(2)}) %collective-permute-start.3) | collective-permute-done | bytes 819232 | tf_op jit(solution)/shard_map/ppermute | solution.py:15
  91.3 0.3 fusion.6
  91.7 3.2 %copy-done = f32[5,640,640]{1,2,0:T(8,128)} copy-done((f32[5,640,640]{1,2,0:T(8,128)}, f32[5,640,640]{1,2,0:T(8,128)S(1)}, u32[]{:S(2)}) %copy-start) | copy-done | bytes 8192024
  94.9 2.0 %add_select_fusion = f32[5,128,128]{1,2,0:T(8,128)S(1)} fusion(f32[5,256,128]{1,2,0:T(8,128)S(1)} %convert_element_type.66, f32[5,640,640]{1,2,0:T(8,128)S(1)} %fusion.24, s32[]{:T(128)} %bitcast.7, s32[]{:T(128)} %bitcast.8, pred[]{:T(512)} %and_reduce_fusion), kind=kLoop, calls=%fused_computation.43 | loop fusion | flops 163840 | bytes 983049 | tf_op jit(solution)/shard_map/select.13
  96.9 5.8 %scatter-add.35 = f32[5,640,640]{1,2,0:T(8,128)} dynamic-update-slice(f32[5,640,640]{1,2,0:T(8,128)} %copy-done, f32[5,128,128]{1,2,0:T(8,128)S(1)} %add_select_fusion, s32[]{:T(128)} %constant.235.clone.1, s32[]{:T(128)} %bitcast.7, s32[]{:T(128)} %bitcast.8) | dynamic-update-slice | bytes 655364 | tf_op jit(solution)/shard_map/scatter-add | solution.py:95
  102.6 1.8 fusion.23
  104.4 1.8 fusion.22
  106.2 7.3 %add_convert_fusion = bf16[5,640,640]{1,2,0:T(8,128)(2,1)S(1)} fusion(f32[5,640,640]{1,2,0:T(8,128)} %fusion.22, s32[5,640,640]{1,2,0:T(8,128)} %copy.19, f32[5]{0:T(128)S(1)} %bitcast.38), kind=kLoop, calls=%fused_computation.4 | loop fusion | flops 10240000 | bytes 20480020 | tf_op jit(solution)/shard_map/convert_element_type | solution.py:99
  113.5 0.3 fusion.42
  113.9 2.3 %collective-permute-start.8 = (bf16[5,128,640]{1,2,0:T(8,128)(2,1)S(1)}, bf16[5,128,640]{1,2,0:T(8,128)(2,1)S(1)}, u32[]{:S(2)}, u32[]{:S(2)}) collective-permute-start(bf16[5,128,640]{1,2,0:T(8,128)(2,1)S(1)} %get-tuple-element.124), channel_id=1, source_target_pairs={{0,4},{4,8},{8,12},{12,16},{16,20},{20,24},{24,28},{1,5},{5,9},{9,... | collective-permute-start | bytes 2457608 | tf_op jit(solution)/shard_map/ppermute | solution.py:26
  116.2 1.5 collective-permute-start.9
  117.7 0.4 collective-permute-done.8
  118.1 5.8 %collective-permute-done.9 = bf16[5,128,640]{1,2,0:T(8,128)(2,1)S(1)} collective-permute-done((bf16[5,128,640]{1,2,0:T(8,128)(2,1)S(1)}, bf16[5,128,640]{1,2,0:T(8,128)(2,1)S(1)}, u32[]{:S(2)}, u32[]{:S(2)}) %collective-permute-start.9) | collective-permute-done | bytes 819232 | tf_op jit(solution)/shard_map/ppermute | solution.py:28
  124.2 4.5 %collective-permute-start.10 = (bf16[5,896,128]{1,2,0:T(8,128)(2,1)S(1)}, bf16[5,896,128]{1,2,0:T(8,128)(2,1)S(1)}, u32[]{:S(2)}, u32[]{:S(2)}) collective-permute-start(bf16[5,896,128]{1,2,0:T(8,128)(2,1)S(1)} %get-tuple-element.122), channel_id=1, source_target_pairs={{0,1},{1,2},{2,3},{4,5},{5,6},{6,7},{8,9},{9,10},{10,11},{12,13},{... | collective-permute-start | bytes 3440648 | tf_op jit(solution)/shard_map/ppermute | solution.py:26
  128.7 1.3 collective-permute-start.11
  130.0 12.0 %collective-permute-done.10 = bf16[5,896,128]{1,2,0:T(8,128)(2,1)S(1)} collective-permute-done((bf16[5,896,128]{1,2,0:T(8,128)(2,1)S(1)}, bf16[5,896,128]{1,2,0:T(8,128)(2,1)S(1)}, u32[]{:S(2)}, u32[]{:S(2)}) %collective-permute-start.10) | collective-permute-done | bytes 1146912 | tf_op jit(solution)/shard_map/ppermute | solution.py:26
  142.0 4.5 %collective-permute-done.11 = bf16[5,896,128]{1,2,0:T(8,128)(2,1)S(1)} collective-permute-done((bf16[5,896,128]{1,2,0:T(8,128)(2,1)S(1)}, bf16[5,896,128]{1,2,0:T(8,128)(2,1)S(1)}, u32[]{:S(2)}, u32[]{:S(2)}) %collective-permute-start.11) | collective-permute-done | bytes 1146912 | tf_op jit(solution)/shard_map/ppermute | solution.py:28
  146.4 5.2 %multiply_reduce_fusion = f32[896,512]{1,0:T(8,128)S(1)} fusion(f32[5,512]{1,0:T(8,128)S(1)} %broadcast_multiply_fusion, f32[512]{0:T(512)S(1)} %mul.154, f32[512]{0:T(512)S(1)} %mul.149, f32[512]{0:T(512)S(1)} %sub.50, f32[896]{0:T(1024)S(1)} %iota_add_fusion, bf16[5,896,128]{1,2,0:T(8,128)(2,1)S(1)} %collective-permute-done.11, ...), kind=kOutput, calls=%fused_computation | convolution fusion | flops 4157440000 | bytes 9883136 | tf_op jit(solution)/shard_map/bij,is->bjs/dot_general | solution.py:104
  151.7 7.7 %multiply_reduce_fusion.2 = (f32[5,512]{1,0:T(8,128)S(1)}, f32[896,512]{1,0:T(8,128)S(1)}) fusion(f32[896,512]{1,0:T(8,128)S(1)} %get-tuple-element.131, f32[5,512]{1,0:T(8,128)S(1)} %broadcast_multiply_fusion, f32[512]{0:T(512)S(1)} %mul.154, f32[512]{0:T(512)S(1)} %mul.149, f32[512]{0:T(512)S(1)} %sub.53, f32[896]{0:T(1024)S(1)} %iota_add_fusion, ...), kind=kOutput, calls=%fused_computation.2 | convolution fusion | flops 4162024960 | bytes 11728384 | tf_op jit(solution)/shard_map/bij,js->bis/dot_general | solution.py:101
  159.4 2.2 %multiply_reduce_fusion.6 = (f32[512]{0:T(512)S(1)}, f32[512]{0:T(512)S(1)}, f32[512]{0:T(512)S(1)}, f32[512]{0:T(512)S(1)}) fusion(f32[896,512]{1,0:T(8,128)S(1)} %get-tuple-element.102, f32[512]{0:T(512)S(1)} %mul.149, f32[512]{0:T(512)S(1)} %sub.50, f32[896]{0:T(1024)S(1)} %iota_add_fusion, f32[512]{0:T(512)S(1)} %mul.154, ...), kind=kLoop, calls=%fused_computation.19 | loop fusion | flops 12843008 | bytes 3689984 | tf_op jit(solution)/shard_map/reduce_sum | solution.py:110
  162.3 32.7 %all_to_all.18 = f32[32,1,128]{2,1,0:T(1,128)S(1)} all-to-all(f32[32,1,128]{2,1,0:T(1,128)S(1)} %reshape.481), channel_id=1, replica_groups=mesh['ra'=8,'dec'=4] {'ra','dec'}, dimensions={0} | all-to-all | bytes 32768 | tf_op jit(solution)/shard_map/all_to_all | solution.py:118
  195.0 0.7 reduce.43
  195.9 1.0 fusion.20
  (55 shorter events, 3.3 us)
Async XLA Ops:
  3.7 19.6 %all-to-all-start = ((f32[32,1,144]{2,1,0:T(1,128)}), f32[32,1,144]{2,1,0:T(1,128)S(1)}, u32[]{:S(2)}, u32[]{:S(2)}) async-start(f32[32,1,144]{2,1,0:T(1,128)} %reshape.479), calls=%async_computation | async-start | bytes 65536 | tf_op jit(solution)/shard_map/all_to_all | solution.py:62
  31.7 10.5 %collective-permute-start.5 = (bf16[5,128,256]{1,2,0:T(8,128)(2,1)S(1)}, bf16[5,128,256]{1,2,0:T(8,128)(2,1)S(1)}, u32[]{:S(2)}, u32[]{:S(2)}) collective-permute-start(bf16[5,128,256]{1,2,0:T(8,128)(2,1)S(1)} %pad_maximum_fusion.5), channel_id=1, source_target_pairs={{0,4},{4,8},{8,12},{12,16},{16,20},{20,24},{24,28},{1,5},{5,9},{9,... | collective-permute-start | bytes 983048 | tf_op jit(solution)/shard_map/ppermute | solution.py:15
  33.9 8.3 %collective-permute-start.4 = (bf16[5,128,256]{1,2,0:T(8,128)(2,1)S(1)}, bf16[5,128,256]{1,2,0:T(8,128)(2,1)S(1)}, u32[]{:S(2)}, u32[]{:S(2)}) collective-permute-start(bf16[5,128,256]{1,2,0:T(8,128)(2,1)S(1)} %pad_maximum_fusion.4), channel_id=1, source_target_pairs={{4,0},{8,4},{12,8},{16,12},{20,16},{24,20},{28,24},{5,1},{9,5},{13... | collective-permute-start | bytes 983048 | tf_op jit(solution)/shard_map/ppermute | solution.py:15
  35.4 38.0 %collective-permute-start.1 = (bf16[5,128,640]{1,2,0:T(8,128)(2,1)S(1)}, bf16[5,128,640]{1,2,0:T(8,128)(2,1)S(1)}, u32[]{:S(2)}, u32[]{:S(2)}) collective-permute-start(bf16[5,128,640]{1,2,0:T(8,128)(2,1)S(1)} %get-tuple-element.120), channel_id=1, source_target_pairs={{0,4},{4,8},{8,12},{12,16},{16,20},{20,24},{24,28},{1,5},{5,9},{9,... | collective-permute-start | bytes 2457608 | tf_op jit(solution)/shard_map/ppermute | solution.py:15
  39.6 33.5 %collective-permute-start = (bf16[5,128,640]{1,2,0:T(8,128)(2,1)S(1)}, bf16[5,128,640]{1,2,0:T(8,128)(2,1)S(1)}, u32[]{:S(2)}, u32[]{:S(2)}) collective-permute-start(bf16[5,128,640]{1,2,0:T(8,128)(2,1)S(1)} %get-tuple-element.121), channel_id=1, source_target_pairs={{4,0},{8,4},{12,8},{16,12},{20,16},{24,20},{28,24},{5,1},{9,5},{13... | collective-permute-start | bytes 2457608 | tf_op jit(solution)/shard_map/ppermute | solution.py:15
  40.9 32.9 %collective-permute-start.2 = (bf16[5,640,128]{1,2,0:T(8,128)(2,1)S(1)}, bf16[5,640,128]{1,2,0:T(8,128)(2,1)S(1)}, u32[]{:S(2)}, u32[]{:S(2)}) collective-permute-start(bf16[5,640,128]{1,2,0:T(8,128)(2,1)S(1)} %get-tuple-element.119), channel_id=1, source_target_pairs={{1,0},{2,1},{3,2},{5,4},{6,5},{7,6},{9,8},{10,9},{11,10},{13,12},{... | collective-permute-start | bytes 2457608 | tf_op jit(solution)/shard_map/ppermute | solution.py:15
  42.3 27.2 %collective-permute-start.6 = (bf16[5,256,128]{1,2,0:T(8,128)(2,1)S(1)}, bf16[5,256,128]{1,2,0:T(8,128)(2,1)S(1)}, u32[]{:S(2)}, u32[]{:S(2)}) collective-permute-start(bf16[5,256,128]{1,2,0:T(8,128)(2,1)S(1)} %pad_maximum_fusion.6), channel_id=1, source_target_pairs={{1,0},{2,1},{3,2},{5,4},{6,5},{7,6},{9,8},{10,9},{11,10},{13,12},{... | collective-permute-start | bytes 983048 | tf_op jit(solution)/shard_map/ppermute | solution.py:15
  43.7 29.3 %collective-permute-start.7 = (bf16[5,256,128]{1,2,0:T(8,128)(2,1)S(1)}, bf16[5,256,128]{1,2,0:T(8,128)(2,1)S(1)}, u32[]{:S(2)}, u32[]{:S(2)}) collective-permute-start(bf16[5,256,128]{1,2,0:T(8,128)(2,1)S(1)} %pad_maximum_fusion.7), channel_id=1, source_target_pairs={{0,1},{1,2},{2,3},{4,5},{5,6},{6,7},{8,9},{9,10},{10,11},{12,13},{... | collective-permute-start | bytes 983048 | tf_op jit(solution)/shard_map/ppermute | solution.py:15
  69.5 21.7 %collective-permute-start.3 = (bf16[5,640,128]{1,2,0:T(8,128)(2,1)S(1)}, bf16[5,640,128]{1,2,0:T(8,128)(2,1)S(1)}, u32[]{:S(2)}, u32[]{:S(2)}) collective-permute-start(bf16[5,640,128]{1,2,0:T(8,128)(2,1)S(1)} %get-tuple-element.118), channel_id=1, source_target_pairs={{0,1},{1,2},{2,3},{4,5},{5,6},{6,7},{8,9},{9,10},{10,11},{12,13},{... | collective-permute-start | bytes 2457608 | tf_op jit(solution)/shard_map/ppermute | solution.py:15
  91.7 3.2 %copy-start = (f32[5,640,640]{1,2,0:T(8,128)}, f32[5,640,640]{1,2,0:T(8,128)S(1)}, u32[]{:S(2)}) copy-start(f32[5,640,640]{1,2,0:T(8,128)S(1)} %fusion.24) | copy-start | bytes 24576004
  91.7 14.5 %copy-start.1 = (f32[1,1,5]{2,1,0:T(1,128)S(1)}, f32[1,1,5]{2,1,0:T(1,128)}, u32[]{:S(2)}) copy-start(f32[1,1,5]{2,1,0:T(1,128)} %param.26) | copy-start | bytes 64
  113.9 4.2 %collective-permute-start.8 = (bf16[5,128,640]{1,2,0:T(8,128)(2,1)S(1)}, bf16[5,128,640]{1,2,0:T(8,128)(2,1)S(1)}, u32[]{:S(2)}, u32[]{:S(2)}) collective-permute-start(bf16[5,128,640]{1,2,0:T(8,128)(2,1)S(1)} %get-tuple-element.124), channel_id=1, source_target_pairs={{0,4},{4,8},{8,12},{12,16},{16,20},{20,24},{24,28},{1,5},{5,9},{9,... | collective-permute-start | bytes 2457608 | tf_op jit(solution)/shard_map/ppermute | solution.py:26
  116.2 7.7 %collective-permute-start.9 = (bf16[5,128,640]{1,2,0:T(8,128)(2,1)S(1)}, bf16[5,128,640]{1,2,0:T(8,128)(2,1)S(1)}, u32[]{:S(2)}, u32[]{:S(2)}) collective-permute-start(bf16[5,128,640]{1,2,0:T(8,128)(2,1)S(1)} %get-tuple-element.125), channel_id=1, source_target_pairs={{4,0},{8,4},{12,8},{16,12},{20,16},{24,20},{28,24},{5,1},{9,5},{13... | collective-permute-start | bytes 2457608 | tf_op jit(solution)/shard_map/ppermute | solution.py:28
  124.2 17.7 %collective-permute-start.10 = (bf16[5,896,128]{1,2,0:T(8,128)(2,1)S(1)}, bf16[5,896,128]{1,2,0:T(8,128)(2,1)S(1)}, u32[]{:S(2)}, u32[]{:S(2)}) collective-permute-start(bf16[5,896,128]{1,2,0:T(8,128)(2,1)S(1)} %get-tuple-element.122), channel_id=1, source_target_pairs={{0,1},{1,2},{2,3},{4,5},{5,6},{6,7},{8,9},{9,10},{10,11},{12,13},{... | collective-permute-start | bytes 3440648 | tf_op jit(solution)/shard_map/ppermute | solution.py:26
  128.7 17.7 %collective-permute-start.11 = (bf16[5,896,128]{1,2,0:T(8,128)(2,1)S(1)}, bf16[5,896,128]{1,2,0:T(8,128)(2,1)S(1)}, u32[]{:S(2)}, u32[]{:S(2)}) collective-permute-start(bf16[5,896,128]{1,2,0:T(8,128)(2,1)S(1)} %get-tuple-element.123), channel_id=1, source_target_pairs={{1,0},{2,1},{3,2},{5,4},{6,5},{7,6},{9,8},{10,9},{11,10},{13,12},{... | collective-permute-start | bytes 3440648 | tf_op jit(solution)/shard_map/ppermute | solution.py:28
  142.0 9.7 %copy-start.2 = (bf16[5,896,128]{1,2,0:T(8,128)(2,1)}, bf16[5,896,128]{1,2,0:T(8,128)(2,1)S(1)}, u32[]{:S(2)}) copy-start(bf16[5,896,128]{1,2,0:T(8,128)(2,1)S(1)} %collective-permute-done.10) | copy-start | bytes 3440644
  146.4 5.2 %copy-start.3 = (bf16[5,896,128]{1,2,0:T(8,128)(2,1)}, bf16[5,896,128]{1,2,0:T(8,128)(2,1)S(1)}, u32[]{:S(2)}) copy-start(bf16[5,896,128]{1,2,0:T(8,128)(2,1)S(1)} %collective-permute-done.11) | copy-start | bytes 3440644
where the time goes:
time: 198 us; the launch traced here: 197 us
  waiting for transfers between devices  59.9 us (30%)
  starting transfers between devices  37 us (19%)
  blocking collectives  32.7 us (17%)
  local copies, waits for them, and re-layouts  23.8 us (12%)
  other arithmetic  22.8 us (12%)
  matrix products  20.1 us (10%)
    ppermute x8, waiting for transfers between devices, passed_along(): lax.ppermute(value, axis, [(source, source + steps) for source in range(l...  37.3 us
    all_to_all x1, blocking collectives, on_device(): lax.all_to_all(slot_grad, ('ra', 'dec'), split_axis=1, concat_axis=1, til...  32.7 us
    ppermute x8, starting transfers between devices, passed_along(): lax.ppermute(value, axis, [(source, source + steps) for source in range(l...  20.2 us
    unnamed x13, local copies, waits for them, and re-layouts  14.5 us
    ppermute x2, waiting for transfers between devices, with_halo(): lax.ppermute(tail, axis, [(i, (i + 1) % count) for i in range(ends)])  12.4 us
    ppermute x2, waiting for transfers between devices, with_halo(): lax.ppermute(head, axis, [((i + 1) % count, i) for i in range(ends)])  10.3 us
    dot_general x1, matrix products, on_device(): jnp.einsum('bij,js->bis', weight_canvas, col_bf, preferred_element_type=j...  7.72 us
    all_to_all x1, starting transfers between devices, on_device(): lax.all_to_all(outgoing, ('ra', 'dec'), split_axis=1, concat_axis=1, tile...  7.3 us
  transfers between devices with their start and end apart: 13, of which 6 were waited for; matrix products, arithmetic and copies ran while one was open for 7% of the time, Pallas kernels for 0%

commit v1 on v0

v1 whole, which is shorter than its diff:
```python
import functools
import math

import jax
import jax.numpy as jnp
from jax import lax
from jax.experimental import pallas as pl
from jax.experimental.pallas import tpu as pltpu
from jax.sharding import PartitionSpec as P

MARGIN = 128
CAT_DEV = 256
BANDS = 5
AXES = ("ra", "dec")
AROUND = [(0, 0), (-1, 0), (1, 0), (0, -1), (0, 1), (-1, -1), (-1, 1), (1, -1), (1, 1)]
EMPTY = -1e30
K = math.sqrt(0.5 * math.log2(math.e))
K2 = 2.0 * math.log(2.0)
F32 = jnp.float32
BF16 = jnp.bfloat16


def dot(a, b):
    return jnp.dot(a, b, preferred_element_type=F32)


def coords(length, first, axis):
    shape = (length, 1) if axis == 0 else (1, length)
    return lax.broadcasted_iota(jnp.int32, shape, axis).astype(F32) + (first + 0.5)


def shape_of(x, center, scale, norm):
    t = (x - center) * scale
    return jnp.exp2(-(t * t)) * norm, t


def params(table, axis):
    def pick(i):
        return table[i : i + 1, :] if axis == 0 else table[:, i : i + 1]

    flux = [jnp.exp(pick(b)) for b in range(BANDS)]
    inverse = jnp.exp(-pick(7)) * (1.0 / MARGIN)
    return flux, pick(5), pick(6), inverse * K, inverse * (1.0 / math.sqrt(2.0 * math.pi)), inverse


def moments(total, x, center, scale, norm, axis):
    p, t = shape_of(x, center, scale, norm)
    q = p * total
    q1 = q * t
    q2 = q1 * t
    return q, q1, q2


def core(side, slots, prm, sky, counts_hbm, out, counts, acc, w, wedge, c_row, c_sc, c_scT, c_col, c_colT,
         v_row, v_sc, v_scT, v_col, v_colT, h_row, h_rowT, h_sc, h_scT, h_colT,
         k_row, k_rowT, k_sc, k_scT, k_colT, big, gsum, hsum, sem):
    M = MARGIN
    rim = side - M
    fetch = pltpu.make_async_copy(counts_hbm, counts, sem)
    fetch.start()

    def table_of(n):
        rows = prm[n]
        return rows, rows.T

    def firsts(di, dj):
        return -di * side, -dj * side

    def span(d):
        return (0, side) if d == 0 else ((0, M) if d < 0 else (rim, M))

    def fill(n, row_at, row_len, col_at, col_len, first_r, first_c, row, rowT, col, colT, scR, scRT, scC, scCT):
        rows, cols = table_of(n)
        flux, rc, cc, scale, norm, _ = params(rows, 0)
        fluxT, rcT, ccT, scaleT, normT, _ = params(cols, 1)
        step = 128

        def by_rows(i, _):
            at = pl.multiple_of(i * step, step)
            p, _t = shape_of(coords(step, (row_at + first_r + i * step).astype(F32), 0), rc, scale, norm)
            if row is not None:
                row[pl.ds(at, step), :] = p.astype(BF16)
            if scR is not None:
                for b in range(BANDS):
                    scR[pl.ds(pl.multiple_of(b * row_len + i * step, step), step), :] = (p * flux[b]).astype(BF16)
            p, _t = shape_of(coords(step, (row_at + first_r + i * step).astype(F32), 1), rcT, scaleT, normT)
            if rowT is not None:
                rowT[:, pl.ds(at, step)] = p.astype(BF16)
            if scRT is not None:
                for b in range(BANDS):
                    scRT[:, pl.ds(pl.multiple_of(b * row_len + i * step, step), step)] = (p * fluxT[b]).astype(BF16)
            return 0

        lax.fori_loop(0, row_len // step, by_rows, 0)

        def by_cols(i, _):
            at = pl.multiple_of(i * step, step)
            p, _t = shape_of(coords(step, (col_at + first_c + i * step).astype(F32), 0), cc, scale, norm)
            if col is not None:
                col[pl.ds(at, step), :] = p.astype(BF16)
            if scC is not None:
                for b in range(BANDS):
                    scC[pl.ds(pl.multiple_of(b * col_len + i * step, step), step), :] = (p * flux[b]).astype(BF16)
            p, _t = shape_of(coords(step, (col_at + first_c + i * step).astype(F32), 1), ccT, scaleT, normT)
            if colT is not None:
                colT[:, pl.ds(at, step)] = p.astype(BF16)
            if scCT is not None:
                for b in range(BANDS):
                    scCT[:, pl.ds(pl.multiple_of(b * col_len + i * step, step), step)] = (p * fluxT[b]).astype(BF16)
            return 0

        lax.fori_loop(0, col_len // step, by_cols, 0)

    zero = jnp.int32(0)
    fill(0, zero, side, zero, side, zero, zero, c_row, None, c_col, c_colT, c_sc, c_scT, None, None)

    def own_band(b, _):
        at = pl.multiple_of(b * side, 128)
        acc[b] = dot(c_sc[pl.ds(at, side), :], c_colT[...])
        return 0

    lax.fori_loop(0, BANDS, own_band, 0)

    def upright(v, _):
        d = 2 * v - 1
        at = pl.multiple_of(v * rim, 128)
        fill(1 + v, at, M, zero, side, -d * side, zero, v_row.at[v], None, v_col.at[v], v_colT.at[v],
             v_sc.at[v], v_scT.at[v], None, None)
        big[...] = dot(v_sc[v], v_colT[v])
        for b in range(BANDS):
            acc[b, pl.ds(at, M), :] += big[b * M : (b + 1) * M, :]
        return 0

    lax.fori_loop(0, 2, upright, 0)

    def sideways(v, _):
        d = 2 * v - 1
        at = pl.multiple_of(v * rim, 128)
        fill(3 + v, zero, side, at, M, zero, -d * side, h_row.at[v], h_rowT.at[v], None, h_colT.at[v],
             None, None, h_sc.at[v], h_scT.at[v])
        big[...] = dot(h_row[v], h_scT[v])
        for b in range(BANDS):
            acc[b, :, pl.ds(at, M)] += big[:, b * M : (b + 1) * M]
        return 0

    lax.fori_loop(0, 2, sideways, 0)

    def corner(v, _):
        vr, vc = v // 2, v % 2
        at_r = pl.multiple_of(vr * rim, 128)
        at_c = pl.multiple_of(vc * rim, 128)
        fill(5 + v, at_r, M, at_c, M, (1 - 2 * vr) * side, (1 - 2 * vc) * side, k_row.at[v], k_rowT.at[v], None,
             k_colT.at[v], None, None, k_sc.at[v], k_scT.at[v])
        big[:M] = dot(k_row[v], k_scT[v])
        for b in range(BANDS):
            acc[b, pl.ds(at_r, M), pl.ds(at_c, M)] += big[:M, b * M : (b + 1) * M]
        return 0

    lax.fori_loop(0, 4, corner, 0)

    fetch.wait()

    for b in range(BANDS):
        level = sky[0, 0, b]

        def band_rows(i, _):
            rows = pl.ds(pl.multiple_of(i * 64, 64), 64)
            ratio = counts[b, rows, :].astype(F32) / (acc[b, rows, :] + level)
            weights = (ratio - 1.0).astype(BF16)
            w[b, rows, :] = weights
            wedge[0, rows, b * M : (b + 1) * M] = weights[:, :M]
            wedge[1, rows, b * M : (b + 1) * M] = weights[:, rim:]
            return 0

        lax.fori_loop(0, side // 64, band_rows, 0)

    def reduce_rows(n, first, length):
        _, rc, _, scale, norm, inverse = params(prm[n], 0)

        def step(i, sums):
            at = pl.multiple_of(i * 64, 64)
            x = coords(64, (first + i * 64).astype(F32), 0)
            q = moments(gsum[pl.ds(at, 64), :], x, rc, scale, norm, 0)
            return tuple(s + jnp.sum(v.reshape(8, 8, slots), axis=0) for s, v in zip(sums, q))

        s0, s1, s2 = lax.fori_loop(0, length // 64, step, (jnp.zeros((8, slots), F32),) * 3)
        s0, s1, s2 = [jnp.sum(s, axis=0, keepdims=True) for s in (s0, s1, s2)]
        return s1 * inverse * (1.0 / K), s2 * K2 - s0

    def reduce_cols(n, first, length, source, extra):
        cols = prm[n].T
        _, _, cc, scale, norm, inverse = params(cols, 1)
        s0 = jnp.zeros((slots, 128), F32)
        s1, s2 = s0, s0
        for i in range(length // 128):
            x = coords(128, first + i * 128, 1)
            q = moments(source[:, i * 128 : (i + 1) * 128], x, cc, scale, norm, 1)
            s0, s1, s2 = s0 + q[0], s1 + q[1], s2 + q[2]
        total = [jnp.sum(s, axis=1, keepdims=True) for s in (s0, s1, s2)]
        lane = lax.broadcasted_iota(jnp.int32, (1, 128), 1)
        found = jnp.where(lane == 6, total[1] * inverse * (1.0 / K), 0.0)
        found = found + jnp.where(lane == 7, total[2] * K2 - total[0], 0.0)
        for m, e in extra:
            found = found + jnp.where(lane == m, e, 0.0)
        return found.T[:8]

    def finish(n, rows, found):
        out[n] = jnp.concatenate(rows, axis=0) + found

    nothing = jnp.zeros((1, slots), F32)

    fl0, _, _, _, _, _ = params(prm[0], 0)
    gsum[...] = jnp.zeros_like(gsum)
    hsum[...] = jnp.zeros_like(hsum)

    own = []
    for b in range(BANDS):
        big[:, :slots] = dot(w[b], c_col[...])

        def own_rows(i, s):
            rows = pl.ds(pl.multiple_of(i * 64, 64), 64)
            a = big[rows, :slots]
            gsum[rows, :] += a * fl0[b]
            return s + jnp.sum((a * c_row[rows, :].astype(F32)).reshape(8, 8, slots), axis=0)

        s = lax.fori_loop(0, side // 64, own_rows, jnp.zeros((8, slots), F32))
        own.append(jnp.sum(s, axis=0, keepdims=True) * fl0[b])
        hsum[...] += dot(c_scT[:, b * side : (b + 1) * side], w[b])
    row_grad, width_r = reduce_rows(0, zero, side)
    found = reduce_cols(0, zero.astype(F32), side, hsum, [])
    finish(0, own + [row_grad, nothing, width_r], found)

    def upright_adjoint(v, _):
        d = 2 * v - 1
        n = 1 + v
        at = pl.multiple_of(v * rim, 128)
        strip = w[:, pl.ds(at, M), :].reshape(BANDS * M, side)
        big[:, :slots] = dot(strip, v_col[v])
        hsum[...] = dot(v_scT[v], strip)
        flux, _, _, _, _, _ = params(prm[n], 0)
        sums = []
        gsum[:M] = jnp.zeros((M, slots), F32)
        for b in range(BANDS):
            a = big[b * M : (b + 1) * M, :slots]
            gsum[:M] += a * flux[b]
            sums.append(jnp.sum(a * v_row[v].astype(F32), axis=0, keepdims=True) * flux[b])
        row_grad, width_r = reduce_rows(n, at - d * side, M)
        found = reduce_cols(n, zero.astype(F32), side, hsum, [])
        finish(n, sums + [row_grad, nothing, width_r], found)
        return 0

    lax.fori_loop(0, 2, upright_adjoint, 0)

    def flat_adjoint(n, strip, rowT, sc, colT, first_r, length, first_c):
        hsum[...] = dot(rowT, strip)
        gsum[:length] = dot(strip, sc)
        fluxT = params(prm[n].T, 1)[0]
        shape = colT.astype(F32)
        total = jnp.zeros((slots, M), F32)
        extra = []
        for b in range(BANDS):
            a = hsum[:, b * M : (b + 1) * M]
            total = total + a * fluxT[b]
            extra.append((b, jnp.sum(a * shape, axis=1, keepdims=True) * fluxT[b]))
        row_grad, width_r = reduce_rows(n, first_r, length)
        hsum[:, :M] = total
        found = reduce_cols(n, first_c, M, hsum, extra)
        finish(n, [nothing] * BANDS + [row_grad, nothing, width_r], found)

    def sideways_adjoint(v, _):
        d = 2 * v - 1
        at = v * rim
        flat_adjoint(3 + v, wedge[v], h_rowT[v], h_sc[v], h_colT[v], zero, side, (at - d * side).astype(F32))
        return 0

    lax.fori_loop(0, 2, sideways_adjoint, 0)

    def corner_adjoint(v, _):
        vr, vc = v // 2, v % 2
        at_r = pl.multiple_of(vr * rim, 128)
        at_c = vc * rim
        flat_adjoint(5 + v, wedge[vc, pl.ds(at_r, M), :], k_rowT[v], k_sc[v], k_colT[v],
                     at_r + (1 - 2 * vr) * side, M, (at_c + (1 - 2 * vc) * side).astype(F32))
        return 0

    lax.fori_loop(0, 4, corner_adjoint, 0)


def render_and_adjoin(prm, sky_level, counts):
    _, side, _ = counts.shape
    slots = prm.shape[2]
    M, B = MARGIN, BANDS
    vm = lambda *s: pltpu.VMEM(s, BF16)
    vf = lambda *s: pltpu.VMEM(s, F32)
    scratch = [
        pltpu.VMEM(counts.shape, counts.dtype), vf(B, side, side), vm(B, side, side), vm(2, side, B * M),
        vm(side, slots), vm(B * side, slots), vm(slots, B * side), vm(side, slots), vm(slots, side),
        vm(2, M, slots), vm(2, B * M, slots), vm(2, slots, B * M), vm(2, side, slots), vm(2, slots, side),
        vm(2, side, slots), vm(2, slots, side), vm(2, B * M, slots), vm(2, slots, B * M), vm(2, slots, M),
        vm(4, M, slots), vm(4, slots, M), vm(4, B * M, slots), vm(4, slots, B * M), vm(4, slots, M),
        vf(side, side), vf(side, slots), vf(slots, side), pltpu.SemaphoreType.DMA,
    ]
    return pl.pallas_call(
        functools.partial(core, side, slots),
        out_shape=jax.ShapeDtypeStruct((9, 8, slots), F32),
        in_specs=[
            pl.BlockSpec(memory_space=pltpu.VMEM),
            pl.BlockSpec(memory_space=pltpu.SMEM),
            pl.BlockSpec(memory_space=pl.ANY),
        ],
        out_specs=pl.BlockSpec(memory_space=pltpu.VMEM),
        scratch_shapes=scratch,
        compiler_params=pltpu.CompilerParams(vmem_limit_bytes=60 * 1024 * 1024),
    )(prm, sky_level, counts)


def on_device(log_flux, position, log_width, owner_tile, sky_level, counts):
    n_ra, n_dec = lax.axis_size("ra"), lax.axis_size("dec")
    tiles = n_ra * n_dec
    cap = max(2, 2 * CAT_DEV // tiles)
    slots = tiles * cap
    here = log_flux.shape[1]
    target = owner_tile[:, 0]
    order = jnp.arange(here, dtype=jnp.int32)
    matches = (target[:, None] == target[None, :]) & (order[None, :] < order[:, None])
    rank = jnp.sum(matches.astype(jnp.int32), axis=1)
    slot = target * cap + rank
    onehot = (slot[:, None] == jnp.arange(slots, dtype=jnp.int32)[None, :]).astype(F32)
    rows = jnp.concatenate([log_flux, position, log_width[None, :], jnp.ones((1, here), F32)], axis=0)
    sorted_rows = jnp.dot(rows, onehot, precision=lax.Precision.HIGHEST)
    sorted_flux = jnp.where(sorted_rows[8:9] > 0.5, sorted_rows[:5], EMPTY)

    def around(x, fill):
        x = jnp.pad(x.reshape(-1, n_ra, n_dec, cap), ((0, 0), (1, 1), (1, 1), (0, 0)), constant_values=fill)
        return jnp.stack([x[:, 1 + i : 1 + i + n_ra, 1 + j : 1 + j + n_dec] for i, j in AROUND])

    outgoing = jnp.concatenate([around(sorted_flux, EMPTY), around(sorted_rows[5:8], 0.0)], axis=1)
    outgoing = outgoing.transpose(2, 3, 1, 0, 4).reshape(tiles, 8, 9 * cap)
    arrived = lax.all_to_all(outgoing, AXES, split_axis=0, concat_axis=0, tiled=True)
    prm = arrived.reshape(tiles, 8, 9, cap).transpose(2, 1, 0, 3).reshape(9, 8, slots)
    grads = render_and_adjoin(prm, sky_level, counts)
    leaving = grads.reshape(9, 8, tiles, cap).transpose(2, 1, 0, 3).reshape(tiles, 8, 9 * cap)
    back = lax.all_to_all(leaving, AXES, split_axis=0, concat_axis=0, tiled=True)
    back = back.reshape(n_ra, n_dec, 8, 9, cap)
    back = jnp.pad(back, ((1, 1), (1, 1), (0, 0), (0, 0), (0, 0)))
    total = sum(back[1 - i : 1 - i + n_ra, 1 - j : 1 - j + n_dec, :, n] for n, (i, j) in enumerate(AROUND))
    total = total.transpose(2, 0, 1, 3).reshape(8, slots)
    return jnp.dot(total, onehot.T, precision=lax.Precision.HIGHEST)


def solution(mesh):
    in_specs = (
        P(None, AXES),
        P(None, AXES),
        P(AXES),
        P(AXES, None),
        P("ra", "dec", None),
        P(None, "ra", "dec"),
    )
    return jax.shard_map(
        on_device, mesh=mesh, in_specs=in_specs, out_specs=P(None, AXES), check_vma=False
    )
```

time: 198 us -> 101 us (0.51)
  waiting for transfers between devices: 59.9 us -> 0 us
  Pallas kernels: 0 us -> 58.8 us
  starting transfers between devices: 37 us -> 0 us
  other arithmetic: 22.8 us -> 2.39 us
  matrix products: 20.1 us -> 2.07 us
  local copies, waits for them, and re-layouts: 23.8 us -> 6.8 us
  blocking collectives: 32.7 us -> 30 us
    ppermute x12 -> x0, waiting for transfers between devices: 59.9 us -> none  [the longest x8 37.3 us: passed_along(): lax.ppermute(value, axis, [(source, source + steps) for source in range(l...]
    pallas_call x0 -> x1, Pallas kernels: none -> 58.8 us  [render_and_adjoin(): pl.pallas_call(functools.partial(core, side, slots), out_shape=jax.ShapeD...]
    ppermute x12 -> x0, starting transfers between devices: 29.7 us -> none  [the longest x8 20.2 us: passed_along(): lax.ppermute(value, axis, [(source, source + steps) for source in range(l...]
    dot_general x5 -> x2, matrix products: 20.1 us -> 2.07 us  [the longest x1 1.06 us: on_device(): sorted_rows = jnp.dot(rows, onehot, precision=lax.Precision.HIGHEST)]
    unnamed x13 -> x16, local copies, waits for them, and re-layouts: 14.5 us -> 0.17 us
    convert_element_type x5 -> x0, other arithmetic: 8.42 us -> none  [the longest x1 7.27 us: on_device(): (counts.astype(jnp.float32) / intensity - 1.0).astype(jnp.bfloat16)]
    all_to_all x1 -> x0, starting transfers between devices: 7.3 us -> none  [on_device(): lax.all_to_all(outgoing, ('ra', 'dec'), split_axis=1, concat_axis=1, tile...]
    scatter-add x1 -> x0, local copies, waits for them, and re-layouts: 5.75 us -> none  [on_device(): interior = interior.at[:, :edge, rim_start:].add(got_left[:, edge:])]
  transfers between devices with their start and end apart: 13 -> 0, of which waited for: 6 -> 0; matrix products, arithmetic and copies ran while one was open for 7% -> 0% of each run, Pallas kernels for 0% -> 0%
where the time goes in v1:
time: 101 us; the launch traced here: 100 us
  Pallas kernels  58.8 us (58%)
  blocking collectives  30 us (30%)
  local copies, waits for them, and re-layouts  6.8 us (7%)
  other arithmetic  2.39 us (2%)
  matrix products  2.07 us (2%)
    pallas_call x1, Pallas kernels, render_and_adjoin(): pl.pallas_call(functools.partial(core, side, slots), out_shape=jax.ShapeD...  58.8 us
    all_to_all x1, blocking collectives, on_device(): lax.all_to_all(outgoing, AXES, split_axis=0, concat_axis=0, tiled=True)  17.3 us
    all_to_all x1, blocking collectives, on_device(): lax.all_to_all(leaving, AXES, split_axis=0, concat_axis=0, tiled=True)  12.7 us

profile of v1, /device:TPU:0, one launch (start us, length us, event | category | flops | bytes accessed | tf_op | source)
XLA Modules:
  0.0 100.4 jit_solution(2508399514791367108)
XLA Ops:
  0.0 0.9 convert_reduce_fusion
  0.9 0.7 multiply_add_fusion
  1.6 0.1 pad.20.clone
  1.7 1.1 %fusion.1 = f32[9,512]{1,0:T(8,128)S(1)} fusion(s32[256]{0:T(256)S(1)} %bitcast.88, f32[1,256]{1,0:T(1,128)} %bitcast.90, f32[2,256]{1,0:T(2,128)} %param.7, f32[5,256]{1,0:T(8,128)} %param.6, f32[9]{0:T(128)S(1)} %pad.20.clone), kind=kOutput, calls=%fused_computation.19 | convolution fusion | flops 14293760 | bytes 27684 | tf_op jit(solution)/shard_map/dot_general | solution.py:330
  2.8 0.1 reshape.36
  2.9 0.1 stack.70
  3.0 0.1 reshape.35
  3.1 0.1 stack.60
  3.6 0.1 maximum_bitcast_fusion
  3.7 0.7 copy.54
  4.5 0.6 reshape.37
  5.0 17.3 %all_to_all.10 = f32[32,8,144]{2,1,0:T(8,128)S(1)} all-to-all(f32[32,8,144]{2,1,0:T(8,128)S(1)} %reshape.37), channel_id=1, replica_groups=mesh['ra'=8,'dec'=4] {'ra','dec'}, dimensions={0} | all-to-all | bytes 294912 | tf_op jit(solution)/shard_map/all_to_all | solution.py:339
  22.3 0.3 copy.55
  22.6 0.4 copy.56
  23.0 1.4 %reshape.39.prm = f32[9,8,512]{2,1,0:T(8,128)} reshape(f32[9,8,32,16]{3,2,1,0:T(8,128)S(1)} %copy.56) | data formatting | bytes 294912 | tf_op jit(solution)/shard_map/reshape | solution.py:340
  24.3 58.8 %shard_map.64 = f32[9,8,512]{2,1,0:T(8,128)} custom-call(f32[9,8,512]{2,1,0:T(8,128)} %reshape.39.prm, f32[1,1,5]{2,1,0:T(1,128)} %sky.1, s32[5,640,640]{2,1,0:T(8,128)} %counts_hbm.1), custom_call_target="tpu_custom_call" | custom-call | tf_op jit(solution)/shard_map/pallas_call | solution.py:303
  83.1 1.3 %reshape.40 = f32[9,8,32,16]{3,2,1,0:T(8,128)S(1)} reshape(f32[9,8,512]{2,1,0:T(8,128)} %shard_map.64) | data formatting | bytes 294912 | tf_op jit(solution)/shard_map/reshape | solution.py:342
  84.5 0.4 copy.57
  84.8 0.3 copy.58
  85.2 12.7 %all_to_all.11 = f32[32,8,144]{2,1,0:T(8,128)S(1)} all-to-all(f32[32,8,144]{2,1,0:T(8,128)S(1)} %copy.58), channel_id=1, replica_groups=mesh['ra'=8,'dec'=4] {'ra','dec'}, dimensions={0} | all-to-all | bytes 294912 | tf_op jit(solution)/shard_map/all_to_all | solution.py:343
  97.9 0.6 reshape.42
  98.5 0.6 fusion.12
  99.2 0.1 reshape.43
  99.3 1.0 %fusion = f32[8,256]{1,0:T(8,128)} fusion(f32[8,512]{1,0:T(8,128)S(1)} %reshape.43, s32[256]{0:T(256)S(1)} %bitcast.89), kind=kOutput, calls=%fused_computation.18 | convolution fusion | flops 12713984 | bytes 25600 | tf_op jit(solution)/shard_map/dot_general | solution.py:348
  (24 shorter events, 0.3 us)

commit v2 on v0

v2 whole, which is shorter than its diff:
```python
import functools
import math

import jax
import jax.numpy as jnp
from jax import lax
from jax.experimental import pallas as pl
from jax.experimental.pallas import tpu as pltpu
from jax.sharding import PartitionSpec as P

MARGIN = 128
CAT_DEV = 256
BANDS = 5
AXES = ("ra", "dec")
AROUND = [(0, 0), (-1, 0), (1, 0), (0, -1), (0, 1), (-1, -1), (-1, 1), (1, -1), (1, 1)]
EMPTY = -1e30
F32 = jnp.float32
BF16 = jnp.bfloat16


def dot(a, b):
    return jnp.dot(a, b, preferred_element_type=F32)


def dot_nt(a, b):
    return lax.dot_general(a, b, (((1,), (1,)), ((), ())), preferred_element_type=F32)


def sources(rows):
    flux = [jnp.exp(rows[b : b + 1]) for b in range(BANDS)]
    inverse = jnp.exp(-rows[7:8]) * (1.0 / MARGIN)
    scale = inverse * inverse * (-0.5 * math.log2(math.e))
    return flux, rows[5:6], rows[6:7], scale, inverse * (1.0 / math.sqrt(2.0 * math.pi)), inverse


def pixels(first, count):
    return lax.broadcasted_iota(jnp.int32, (count, 1), 0).astype(F32) + first


def fill_long(ref, length, first, center, scale, norm):
    step = 64

    def body(i, _):
        d = pixels(first + (i * step).astype(F32), step) - center
        ref[pl.ds(pl.multiple_of(i * step, step), step), :] = (jnp.exp2(d * (d * scale)) * norm).astype(BF16)
        return 0

    lax.fori_loop(0, length // step, body, 0)


def fill_short(ref, scaled, first, center, scale, norm, flux):
    step = 32
    peaks = [norm * f for f in flux]

    def body(i, _):
        d = pixels(first + (i * step).astype(F32), step) - center
        e = jnp.exp2(d * (d * scale))
        ref[pl.ds(pl.multiple_of(i * step, step), step), :] = (e * norm).astype(BF16)
        for b in range(BANDS):
            scaled[pl.ds(pl.multiple_of(b * MARGIN + i * step, step), step), :] = (e * peaks[b]).astype(BF16)
        return 0

    lax.fori_loop(0, MARGIN // step, body, 0)


def fold(x):
    total = x[:8]
    for i in range(8, x.shape[0], 8):
        total = total + x[i : i + 8]
    return total


def moments(total, first, center, scale):
    d = pixels(first, total.shape[0]) - center
    q = jnp.exp2(d * (d * scale)) * total
    q1 = q * d
    return fold(q), fold(q1), fold(q1 * d)


def reduce_short(buf, shape, first, center, scale, flux, width=256, step=16):
    slots = buf.shape[1]
    parts = []
    for lo in range(0, slots, width):
        lanes = slice(lo, lo + width)
        sums = None
        for r in range(0, MARGIN, step):
            p = shape[r : r + step, lanes].astype(F32)
            new = []
            total = None
            for b in range(BANDS):
                a = buf[b * MARGIN + r : b * MARGIN + r + step, lanes]
                new.append(fold(a * p))
                a = a * flux[b][:, lanes]
                total = a if total is None else total + a
            new.extend(moments(total, first + r, center[:, lanes], scale[:, lanes]))
            sums = new if sums is None else [s + v for s, v in zip(sums, new)]
        parts.append(sums)
    return [jnp.concatenate([p[m] for p in parts], axis=1) for m in range(BANDS + 3)]


def reduce_long(buf, length, first, center, scale, width=256, step=16):
    slots = buf.shape[1]
    parts = []
    for lo in range(0, slots, width):
        lanes = slice(lo, lo + width)
        sums = None
        for r in range(0, length, step):
            new = moments(buf[r : r + step, lanes], first + r, center[:, lanes], scale[:, lanes])
            sums = new if sums is None else [s + v for s, v in zip(sums, new)]
        parts.append(sums)
    return [jnp.concatenate([p[m] for p in parts], axis=1) for m in range(3)]


def slopes(m, norm, inverse):
    m = [jnp.sum(v, axis=0, keepdims=True) for v in m]
    square = inverse * inverse
    return norm * square * m[1], norm * (square * m[2] - m[0])


def core(side, prm, sky, counts_hbm, out, counts, w, wt, flat, strip, rim_sum,
         c_row, c_sc, c_col, e_short, e_sc, e_long, k_short, k_sc, k_long, big, xbuf, ybuf, sem):
    M = MARGIN
    chunks = side // M
    last = side - M
    fetch = pltpu.make_async_copy(counts_hbm, counts, sem)
    fetch.start()

    flux, rc, cc, scale, norm, inverse = sources(prm[0])
    fill_long(c_col, side, 0.5, cc, scale, norm)

    def own_fill(c, _):
        fill_short(c_row.at[c], c_sc.at[c], (c * M).astype(F32) + 0.5, rc, scale, norm, flux)
        return 0

    lax.fori_loop(0, chunks, own_fill, 0)

    def edge_at(e):
        return jnp.where(e % 2 == 0, side, -M).astype(F32) + 0.5

    def edge_fill(e, _):
        flux, rc, cc, scale, norm, inverse = sources(prm[1 + e])
        across = jnp.where(e < 2, rc, cc)
        along = jnp.where(e < 2, cc, rc)
        fill_short(e_short.at[e], e_sc.at[e], edge_at(e), across, scale, norm, flux)
        fill_long(e_long.at[e], side, 0.5, along, scale, norm)
        return 0

    lax.fori_loop(0, 4, edge_fill, 0)

    def corner_fill(k, _):
        flux, rc, cc, scale, norm, inverse = sources(prm[5 + k])
        fill_short(k_short.at[k], k_sc.at[k], edge_at(k), cc, scale, norm, flux)
        fill_long(k_long.at[k], M, edge_at(k // 2), rc, scale, norm)
        return 0

    lax.fori_loop(0, 4, corner_fill, 0)

    def rim_render(v, _):
        rim_sum[v] = dot_nt(e_long[2 + v], e_sc[2 + v])
        rim_sum[v, :M] += dot_nt(k_long[v], k_sc[v])
        rim_sum[v, last:] += dot_nt(k_long[2 + v], k_sc[2 + v])
        return 0

    lax.fori_loop(0, 2, rim_render, 0)

    fetch.wait()

    def own_render(c, _):
        big[...] = dot_nt(c_sc[c], c_col[...])

        @pl.when((c == 0) | (c == chunks - 1))
        def _():
            v = jnp.where(c == 0, 0, 1)
            big[...] += dot_nt(e_sc[v], e_long[v])

        rows = pl.ds(pl.multiple_of(c * M, M), M)
        for b in range(BANDS):
            band = slice(b * M, (b + 1) * M)
            level = sky[0, 0, b]
            seen = counts[b, rows, :].astype(F32)
            left = big[band, :M] + rim_sum[0, rows, band]
            right = big[band, last:] + rim_sum[1, rows, band]
            model = jnp.concatenate([left, big[band, M:last], right], axis=1)
            weights = (seen / (model + level) - 1.0).astype(BF16)
            turned = weights.T
            w[c, band, :] = weights
            wt[c, :, band] = turned
            flat[0, rows, band] = weights[:, :M]
            flat[1, rows, band] = weights[:, last:]
            strip[0, band, rows] = turned[:M]
            strip[1, band, rows] = turned[last:]
        return 0

    lax.fori_loop(0, chunks, own_render, 0)

    def own_adjoint(c, sums):
        xbuf[...] = dot(w[c], c_col[...])
        found = reduce_short(xbuf, c_row.at[c], (c * M).astype(F32) + 0.5, rc, scale, flux)

        @pl.when(c == 0)
        def _():
            ybuf[...] = dot(wt[c], c_sc[c])

        @pl.when(c > 0)
        def _():
            ybuf[...] += dot(wt[c], c_sc[c])

        return tuple(s + f for s, f in zip(sums, found))

    slots = prm.shape[2]
    found = lax.fori_loop(0, chunks, own_adjoint, (jnp.zeros((8, slots), F32),) * (BANDS + 3))
    nothing = jnp.zeros((1, slots), F32)
    sums = [jnp.sum(s, axis=0, keepdims=True) * f for s, f in zip(found[:BANDS], flux)]
    row_grad, width_r = slopes(found[BANDS:], norm, inverse)
    col_grad, width_c = slopes(reduce_long(ybuf, side, 0.5, cc, scale), norm, inverse)
    out[0] = jnp.concatenate(sums + [row_grad, col_grad, width_r + width_c], axis=0)

    def edge_adjoint(e, _):
        flux, rc, cc, scale, norm, inverse = sources(prm[1 + e])
        across = jnp.where(e < 2, rc, cc)
        along = jnp.where(e < 2, cc, rc)

        @pl.when(e < 2)
        def _():
            c = jnp.where(e == 0, 0, chunks - 1)
            xbuf[...] = dot(w[c], e_long[e])
            ybuf[...] = dot(wt[c], e_sc[e])

        @pl.when(e >= 2)
        def _():
            xbuf[...] = dot(strip[e - 2], e_long[e])
            ybuf[...] = dot(flat[e - 2], e_sc[e])

        found = reduce_short(xbuf, e_short.at[e], edge_at(e), across, scale, flux)
        sums = [jnp.sum(s, axis=0, keepdims=True) * f for s, f in zip(found[:BANDS], flux)]
        across_grad, width_a = slopes(found[BANDS:], norm, inverse)
        along_grad, width_b = slopes(reduce_long(ybuf, side, 0.5, along, scale), norm, inverse)
        row_grad = jnp.where(e < 2, across_grad, along_grad)
        col_grad = jnp.where(e < 2, along_grad, across_grad)
        out[1 + e] = jnp.concatenate(sums + [row_grad, col_grad, width_a + width_b], axis=0)
        return 0

    lax.fori_loop(0, 4, edge_adjoint, 0)

    def corner_adjoint(k, _):
        flux, rc, cc, scale, norm, inverse = sources(prm[5 + k])
        v = k % 2
        at = pl.multiple_of((k // 2) * last, M)
        xbuf[...] = dot(strip[v, :, pl.ds(at, M)], k_long[k])
        ybuf[:M] = dot(flat[v, pl.ds(at, M), :], k_sc[k])
        found = reduce_short(xbuf, k_short.at[k], edge_at(k), cc, scale, flux)
        sums = [jnp.sum(s, axis=0, keepdims=True) * f for s, f in zip(found[:BANDS], flux)]
        col_grad, width_c = slopes(found[BANDS:], norm, inverse)
        row_grad, width_r = slopes(reduce_long(ybuf, M, edge_at(k // 2), rc, scale), norm, inverse)
        out[5 + k] = jnp.concatenate(sums + [row_grad, col_grad, width_r + width_c], axis=0)
        return 0

    lax.fori_loop(0, 4, corner_adjoint, 0)


def render_and_adjoin(prm, sky_level, counts):
    _, side, _ = counts.shape
    slots = prm.shape[2]
    M, B = MARGIN, BANDS
    chunks = side // M
    vm = lambda *s: pltpu.VMEM(s, BF16)
    vf = lambda *s: pltpu.VMEM(s, F32)
    scratch = [
        pltpu.VMEM(counts.shape, counts.dtype),
        vm(chunks, B * M, side), vm(chunks, side, B * M), vm(2, side, B * M), vm(2, B * M, side), vf(2, side, B * M),
        vm(chunks, M, slots), vm(chunks, B * M, slots), vm(side, slots),
        vm(4, M, slots), vm(4, B * M, slots), vm(4, side, slots),
        vm(4, M, slots), vm(4, B * M, slots), vm(4, M, slots),
        vf(B * M, side), vf(B * M, slots), vf(side, slots), pltpu.SemaphoreType.DMA,
    ]
    return pl.pallas_call(
        functools.partial(core, side),
        out_shape=jax.ShapeDtypeStruct((9, 8, slots), F32),
        in_specs=[
            pl.BlockSpec(memory_space=pltpu.VMEM),
            pl.BlockSpec(memory_space=pltpu.SMEM),
            pl.BlockSpec(memory_space=pl.ANY),
        ],
        out_specs=pl.BlockSpec(memory_space=pltpu.VMEM),
        scratch_shapes=scratch,
        compiler_params=pltpu.CompilerParams(vmem_limit_bytes=60 * 1024 * 1024),
    )(prm, sky_level, counts)


def on_device(log_flux, position, log_width, owner_tile, sky_level, counts):
    n_ra, n_dec = lax.axis_size("ra"), lax.axis_size("dec")
    tiles = n_ra * n_dec
    cap = max(2, 2 * CAT_DEV // tiles)
    slots = tiles * cap
    here = log_flux.shape[1]
    target = owner_tile[:, 0]
    order = jnp.arange(here, dtype=jnp.int32)
    matches = (target[:, None] == target[None, :]) & (order[None, :] < order[:, None])
    rank = jnp.sum(matches.astype(jnp.int32), axis=1)
    slot = target * cap + rank
    onehot = (slot[:, None] == jnp.arange(slots, dtype=jnp.int32)[None, :]).astype(F32)
    rows = jnp.concatenate([log_flux, position, log_width[None, :], jnp.ones((1, here), F32)], axis=0)
    sorted_rows = jnp.dot(rows, onehot, precision=lax.Precision.HIGHEST)
    sorted_flux = jnp.where(sorted_rows[8:9] > 0.5, sorted_rows[:5], EMPTY)

    def around(x, fill):
        x = jnp.pad(x.reshape(-1, n_ra, n_dec, cap), ((0, 0), (1, 1), (1, 1), (0, 0)), constant_values=fill)
        return jnp.stack([x[:, 1 + i : 1 + i + n_ra, 1 + j : 1 + j + n_dec] for i, j in AROUND])

    outgoing = jnp.concatenate([around(sorted_flux, EMPTY), around(sorted_rows[5:8], 0.0)], axis=1)
    outgoing = outgoing.transpose(2, 3, 1, 0, 4).reshape(tiles, 8, 9 * cap)
    arrived = lax.all_to_all(outgoing, AXES, split_axis=0, concat_axis=0, tiled=True)
    prm = arrived.reshape(tiles, 8, 9, cap).transpose(2, 1, 0, 3).reshape(9, 8, slots)
    grads = render_and_adjoin(prm, sky_level, counts)
    leaving = grads.reshape(9, 8, tiles, cap).transpose(2, 1, 0, 3).reshape(tiles, 8, 9 * cap)
    back = lax.all_to_all(leaving, AXES, split_axis=0, concat_axis=0, tiled=True)
    back = back.reshape(n_ra, n_dec, 8, 9, cap)
    back = jnp.pad(back, ((1, 1), (1, 1), (0, 0), (0, 0), (0, 0)))
    total = sum(back[1 - i : 1 - i + n_ra, 1 - j : 1 - j + n_dec, :, n] for n, (i, j) in enumerate(AROUND))
    total = total.transpose(2, 0, 1, 3).reshape(8, slots)
    return jnp.dot(total, onehot.T, precision=lax.Precision.HIGHEST)


def solution(mesh):
    in_specs = (
        P(None, AXES),
        P(None, AXES),
        P(AXES),
        P(AXES, None),
        P("ra", "dec", None),
        P(None, "ra", "dec"),
    )
    return jax.shard_map(
        on_device, mesh=mesh, in_specs=in_specs, out_specs=P(None, AXES), check_vma=False
    )
```

time: 198 us -> 75.5 us (0.38)
  waiting for transfers between devices: 59.9 us -> 0 us
  starting transfers between devices: 37 us -> 0 us
  Pallas kernels: 0 us -> 33.7 us
  other arithmetic: 22.8 us -> 2.39 us
  matrix products: 20.1 us -> 2.07 us
  local copies, waits for them, and re-layouts: 23.8 us -> 6.8 us
  blocking collectives: 32.7 us -> 30 us
    ppermute x12 -> x0, waiting for transfers between devices: 59.9 us -> none  [the longest x8 37.3 us: passed_along(): lax.ppermute(value, axis, [(source, source + steps) for source in range(l...]
    pallas_call x0 -> x1, Pallas kernels: none -> 33.7 us  [render_and_adjoin(): pl.pallas_call(functools.partial(core, side), out_shape=jax.ShapeDtypeStr...]
    ppermute x12 -> x0, starting transfers between devices: 29.7 us -> none  [the longest x8 20.2 us: passed_along(): lax.ppermute(value, axis, [(source, source + steps) for source in range(l...]
    dot_general x5 -> x2, matrix products: 20.1 us -> 2.07 us  [the longest x1 1.06 us: on_device(): sorted_rows = jnp.dot(rows, onehot, precision=lax.Precision.HIGHEST)]
    unnamed x13 -> x16, local copies, waits for them, and re-layouts: 14.5 us -> 0.17 us
    convert_element_type x5 -> x0, other arithmetic: 8.42 us -> none  [the longest x1 7.27 us: on_device(): (counts.astype(jnp.float32) / intensity - 1.0).astype(jnp.bfloat16)]
    all_to_all x1 -> x0, starting transfers between devices: 7.3 us -> none  [on_device(): lax.all_to_all(outgoing, ('ra', 'dec'), split_axis=1, concat_axis=1, tile...]
    scatter-add x1 -> x0, local copies, waits for them, and re-layouts: 5.75 us -> none  [on_device(): interior = interior.at[:, :edge, rim_start:].add(got_left[:, edge:])]
  transfers between devices with their start and end apart: 13 -> 0, of which waited for: 6 -> 0; matrix products, arithmetic and copies ran while one was open for 7% -> 0% of each run, Pallas kernels for 0% -> 0%
where the time goes in v2:
time: 75.5 us; the launch traced here: 75.2 us
  Pallas kernels  33.7 us (45%)
  blocking collectives  30 us (40%)
  local copies, waits for them, and re-layouts  6.8 us (9%)
  other arithmetic  2.39 us (3%)
  matrix products  2.07 us (3%)
    pallas_call x1, Pallas kernels, render_and_adjoin(): pl.pallas_call(functools.partial(core, side), out_shape=jax.ShapeDtypeStr...  33.7 us
    all_to_all x1, blocking collectives, on_device(): lax.all_to_all(outgoing, AXES, split_axis=0, concat_axis=0, tiled=True)  17.3 us
    all_to_all x1, blocking collectives, on_device(): lax.all_to_all(leaving, AXES, split_axis=0, concat_axis=0, tiled=True)  12.7 us
    reshape x2, local copies, waits for them, and re-layouts, on_device(): grads.reshape(9, 8, tiles, cap).transpose(2, 1, 0, 3)  1.66 us

profile of v2, /device:TPU:0, one launch (start us, length us, event | category | flops | bytes accessed | tf_op | source)
XLA Modules:
  0.0 75.2 jit_solution(11180460911657410703)
XLA Ops:
  0.0 0.9 %convert_reduce_fusion = s32[256]{0:T(256)S(1)} fusion(s32[256]{0:T(256)} %bitcast.86), kind=kLoop, calls=%fused_computation.30 | loop fusion | flops 327424 | bytes 2048 | tf_op jit(solution)/shard_map/reduce_sum | solution.py:299
  0.9 0.7 multiply_add_fusion
  1.6 0.1 pad.20.clone
  1.7 1.1 %fusion.1 = f32[9,512]{1,0:T(8,128)S(1)} fusion(s32[256]{0:T(256)S(1)} %bitcast.88, f32[1,256]{1,0:T(1,128)} %bitcast.90, f32[2,256]{1,0:T(2,128)} %param.7, f32[5,256]{1,0:T(8,128)} %param.6, f32[9]{0:T(128)S(1)} %pad.20.clone), kind=kOutput, calls=%fused_computation.19 | convolution fusion | flops 14293760 | bytes 27684 | tf_op jit(solution)/shard_map/dot_general | solution.py:303
  2.8 0.1 reshape.36
  2.9 0.1 stack.70
  3.0 0.1 reshape.35
  3.1 0.1 stack.60
  3.6 0.1 maximum_bitcast_fusion
  3.7 0.7 copy.54
  4.5 0.6 reshape.37
  5.0 17.3 %all_to_all.10 = f32[32,8,144]{2,1,0:T(8,128)S(1)} all-to-all(f32[32,8,144]{2,1,0:T(8,128)S(1)} %reshape.37), channel_id=1, replica_groups=mesh['ra'=8,'dec'=4] {'ra','dec'}, dimensions={0} | all-to-all | bytes 294912 | tf_op jit(solution)/shard_map/all_to_all | solution.py:312
  22.3 0.3 copy.55
  22.6 0.4 copy.56
  23.0 1.4 %reshape.39.prm = f32[9,8,512]{2,1,0:T(8,128)} reshape(f32[9,8,32,16]{3,2,1,0:T(8,128)S(1)} %copy.56) | data formatting | bytes 294912 | tf_op jit(solution)/shard_map/reshape | solution.py:313
  24.3 33.7 %shard_map.64 = f32[9,8,512]{2,1,0:T(8,128)} custom-call(f32[9,8,512]{2,1,0:T(8,128)} %reshape.39.prm, f32[1,1,5]{2,1,0:T(1,128)} %sky.1, s32[5,640,640]{2,1,0:T(8,128)} %counts_hbm.1), custom_call_target="tpu_custom_call" | custom-call | tf_op jit(solution)/shard_map/pallas_call | solution.py:276
  58.0 1.3 %reshape.40 = f32[9,8,32,16]{3,2,1,0:T(8,128)S(1)} reshape(f32[9,8,512]{2,1,0:T(8,128)} %shard_map.64) | data formatting | bytes 294912 | tf_op jit(solution)/shard_map/reshape | solution.py:315
  59.3 0.4 copy.57
  59.7 0.3 copy.58
  60.0 12.7 %all_to_all.11 = f32[32,8,144]{2,1,0:T(8,128)S(1)} all-to-all(f32[32,8,144]{2,1,0:T(8,128)S(1)} %copy.58), channel_id=1, replica_groups=mesh['ra'=8,'dec'=4] {'ra','dec'}, dimensions={0} | all-to-all | bytes 294912 | tf_op jit(solution)/shard_map/all_to_all | solution.py:316
  72.8 0.6 reshape.42
  73.4 0.6 fusion.12
  74.1 0.1 reshape.43
  74.2 1.0 %fusion = f32[8,256]{1,0:T(8,128)} fusion(f32[8,512]{1,0:T(8,128)S(1)} %reshape.43, s32[256]{0:T(256)S(1)} %bitcast.89), kind=kOutput, calls=%fused_computation.18 | convolution fusion | flops 12713984 | bytes 25600 | tf_op jit(solution)/shard_map/dot_general | solution.py:321
  (24 shorter events, 0.3 us)

commit v3 on v2

v3 whole, which is shorter than its diff:
```python
import functools
import math

import jax
import jax.numpy as jnp
from jax import lax
from jax.experimental import pallas as pl
from jax.experimental.pallas import tpu as pltpu
from jax.sharding import PartitionSpec as P

MARGIN = 128
CAT_DEV = 256
BANDS = 5
AXES = ("ra", "dec")
AROUND = [(0, 0), (-1, 0), (1, 0), (0, -1), (0, 1), (-1, -1), (-1, 1), (1, -1), (1, 1)]
EMPTY = -1e30
F32 = jnp.float32
BF16 = jnp.bfloat16


def dot(a, b):
    return jnp.dot(a, b, preferred_element_type=F32)


def dot_nt(a, b):
    return lax.dot_general(a, b, (((1,), (1,)), ((), ())), preferred_element_type=F32)


def dot_tn(a, b):
    return lax.dot_general(a, b, (((0,), (0,)), ((), ())), preferred_element_type=F32)


def sources(rows):
    flux = [jnp.exp(rows[b : b + 1]) for b in range(BANDS)]
    inverse = jnp.exp(-rows[7:8]) * (1.0 / MARGIN)
    scale = inverse * inverse * (-0.5 * math.log2(math.e))
    return flux, rows[5:6], rows[6:7], scale, inverse * (1.0 / math.sqrt(2.0 * math.pi)), inverse


def distance(first, count, center):
    return lax.broadcasted_iota(jnp.int32, (count, 1), 0).astype(F32) + first - center


def fill_long(ref, length, first, center, scale, norm, step=32, width=128):
    for lo in range(0, ref.shape[1], width):
        lanes = slice(lo, lo + width)
        d0 = distance(first, step, center[:, lanes])
        for r in range(0, length, step):
            d = d0 + float(r)
            ref[r : r + step, lanes] = (jnp.exp2(d * (d * scale[:, lanes])) * norm[:, lanes]).astype(BF16)


def fill_scaled(ref, first, center, scale, norm, flux, step=32, width=128):
    for lo in range(0, ref.shape[1], width):
        lanes = slice(lo, lo + width)
        d0 = distance(first, step, center[:, lanes])
        peaks = [norm[:, lanes] * f[:, lanes] for f in flux]
        for r in range(0, MARGIN, step):
            d = d0 + float(r)
            e = jnp.exp2(d * (d * scale[:, lanes]))
            for b in range(BANDS):
                ref[b * MARGIN + r : b * MARGIN + r + step, lanes] = (e * peaks[b]).astype(BF16)


def fold(x):
    total = x[:8]
    for i in range(8, x.shape[0], 8):
        total = total + x[i : i + 8]
    return total


def reduce_short(buf, first, center, scale, flux, step=32, width=128):
    parts = []
    for lo in range(0, buf.shape[1], width):
        lanes = slice(lo, lo + width)
        fluxes = [f[:, lanes] for f in flux]
        d0 = distance(first, step, center[:, lanes])
        sums = None
        for r in range(0, MARGIN, step):
            d = d0 + float(r)
            e = jnp.exp2(d * (d * scale[:, lanes]))
            new = []
            total = None
            for b in range(BANDS):
                a = buf[b * MARGIN + r : b * MARGIN + r + step, lanes] * e
                new.append(fold(a))
                a = a * fluxes[b]
                total = a if total is None else total + a
            q = total * d
            new.extend([fold(q), fold(q * d)])
            sums = new if sums is None else [s + v for s, v in zip(sums, new)]
        parts.append(sums)
    found = [jnp.concatenate([p[m] for p in parts], axis=1) for m in range(BANDS + 2)]
    return [found[m] * flux[m] for m in range(BANDS)] + found[BANDS:]


def reduce_long(buf, length, first, center, scale, step=32, width=128):
    parts = []
    for lo in range(0, buf.shape[1], width):
        lanes = slice(lo, lo + width)
        d0 = distance(first, step, center[:, lanes])
        sums = None
        for r in range(0, length, step):
            d = d0 + float(r)
            q = jnp.exp2(d * (d * scale[:, lanes])) * buf[r : r + step, lanes]
            q1 = q * d
            new = [fold(q), fold(q1), fold(q1 * d)]
            sums = new if sums is None else [s + v for s, v in zip(sums, new)]
        parts.append(sums)
    return [jnp.concatenate([p[m] for p in parts], axis=1) for m in range(3)]


def settle(short, long, norm, inverse):
    short = [jnp.sum(v, axis=0, keepdims=True) * norm for v in short]
    long = [jnp.sum(v, axis=0, keepdims=True) * norm for v in long]
    square = inverse * inverse
    bands = short[:BANDS]
    zeroth = bands[0] + bands[1] + bands[2] + bands[3] + bands[4]
    width = square * short[BANDS + 1] - zeroth + (square * long[2] - long[0])
    return bands, square * short[BANDS], square * long[1], width


def core(side, cap, arrived, sky, counts_hbm, leaving, prm, out, counts, canvas, w, w_next, side_w, rim_sum,
         c_sc, c_col, e_sc, e_long, k_sc, k_long, xa, xb, yb, yk, sem):
    M = MARGIN
    chunks = side // M
    last = side - M
    fetch = pltpu.make_async_copy(counts_hbm, counts, sem)
    fetch.start()
    tiles = arrived.shape[0] // 9
    slots = prm.shape[2]
    for n in range(9):
        table = arrived[pl.ds(n, tiles, stride=9), :].T
        prm[n] = jnp.concatenate([table[8 * r : 8 * r + 8] for r in range(cap)], axis=1)

    def number(c):
        return c.astype(F32) * float(M) + 0.5

    flux, rc, cc, scale, norm, inverse = sources(prm[0])

    def col_fill(c, _):
        at = pl.multiple_of(c * M, M)
        fill_long(c_col.at[pl.ds(at, M), :], M, number(c), cc, scale, norm)
        fill_scaled(c_sc.at[c], number(c), rc, scale, norm, flux)
        return 0

    lax.fori_loop(0, chunks, col_fill, 0)

    def edge_fill(e, across_is_row, at, index):
        flux, rc, cc, scale, norm, _ = sources(prm[index])
        across = jnp.where(across_is_row, rc, cc)
        along = jnp.where(across_is_row, cc, rc)
        fill_scaled(e_sc.at[e], at, across, scale, norm, flux)
        fill_long(e_long.at[e], side, 0.5, along, scale, norm)

    def corner_fill(k, left, v):
        flux, rc, cc, scale, norm, _ = sources(prm[5 + k])
        fill_scaled(k_sc.at[k], (side if left else -M) + 0.5, cc, scale, norm, flux)
        fill_long(k_long.at[k], M, jnp.where(v == 0, side, -M).astype(F32) + 0.5, rc, scale, norm)

    def own_render(c, _):
        canvas[c] = dot_nt(c_sc[c], c_col[...])
        edge_fill(c, c < 2, jnp.where(c % 2 == 0, side, -M).astype(F32) + 0.5, 1 + c)
        return 0

    lax.fori_loop(0, 4, own_render, 0)

    def more_render(c, _):
        canvas[c] = dot_nt(c_sc[c], c_col[...])
        return 0

    lax.fori_loop(4, chunks, more_render, 0)

    def rim_render(v, _):
        rim_sum[v] = dot_nt(e_long[2 + v], e_sc[2 + v])
        corner_fill(2 * v, True, v)
        corner_fill(2 * v + 1, False, v)
        return 0

    lax.fori_loop(0, 2, rim_render, 0)

    fetch.wait()

    def weigh(c, own):
        rows = pl.ds(pl.multiple_of(c * M, M), M)
        for b in range(BANDS):
            band = slice(b * M, (b + 1) * M)
            level = sky[0, 0, b]
            seen = counts[b, rows, :].astype(F32)
            left = canvas[c, band, :M] + rim_sum[0, rows, band]
            right = canvas[c, band, last:] + rim_sum[1, rows, band]
            model = jnp.concatenate([left, canvas[c, band, M:last], right], axis=1)
            weights = (seen / (model + level) - 1.0).astype(BF16)
            own[band, :] = weights
            side_w[0, band, rows] = weights[:, :M].T
            side_w[1, band, rows] = weights[:, last:].T

    def end_render(v, _):
        at = pl.ds(pl.multiple_of(v * last, M), M)
        rim_sum[0, at] += dot_nt(k_long[2 * v], k_sc[2 * v])
        rim_sum[1, at] += dot_nt(k_long[2 * v + 1], k_sc[2 * v + 1])
        canvas[v * (chunks - 1)] += dot_nt(e_sc[v], e_long[v])
        return 0

    lax.fori_loop(0, 2, end_render, 0)
    weigh(jnp.int32(0), w.at[0])

    yb[...] = jnp.zeros_like(yb)

    def own_adjoint(c, sums):
        xa[...] = dot(w[c], c_col[...])
        yb[...] += dot_tn(w[c], c_sc[c])
        later = jnp.minimum(c + 1, chunks - 1)
        weigh(later, w_next)
        found = reduce_short(xa, number(c), rc, scale, flux)
        w[later] = w_next[...]
        return tuple(s + f for s, f in zip(sums, found))

    short = lax.fori_loop(0, chunks, own_adjoint, (jnp.zeros((8, slots), F32),) * (BANDS + 2))
    w[chunks] = side_w[0]
    w[chunks + 1] = side_w[1]

    def settle_tile(g, short):
        _, rc, cc, scale, norm, inverse = sources(prm[g])
        rows_short = g < 3
        long = reduce_long(yb, side, 0.5, jnp.where(rows_short, cc, rc), scale)
        bands, across, along, width = settle(short, long, norm, inverse)
        row_grad = jnp.where(rows_short, across, along)
        col_grad = jnp.where(rows_short, along, across)
        out[g] = jnp.concatenate(bands + [row_grad, col_grad, width], axis=0)

    def settle_corner(k):
        flux, rc, cc, scale, norm, inverse = sources(prm[5 + k])
        found = reduce_short(xb, jnp.where(k % 2 == 0, side, -M).astype(F32) + 0.5, cc, scale, flux)
        long = reduce_long(yk, M, jnp.where(k < 2, side, -M).astype(F32) + 0.5, rc, scale)
        bands, col_grad, row_grad, width = settle(found, long, norm, inverse)
        out[5 + k] = jnp.concatenate(bands + [row_grad, col_grad, width], axis=0)

    def edge_adjoint(e, short):
        settle_corner(e - 1)
        settle_tile(e, short)
        v, at = e % 2, pl.ds(pl.multiple_of(e // 2 * last, M), M)
        strip = jnp.where(e == 0, 0, e + chunks - 2)
        xa[...] = dot(w[strip], e_long[e])
        xb[...] = dot(w[chunks + v, :, at], k_long[e])
        yk[...] = dot_tn(w[chunks + v, :, at], k_sc[e])
        yb[...] = dot_tn(w[strip], e_sc[e])
        flux, rc, cc, scale, _, _ = sources(prm[1 + e])
        first = jnp.where(v == 0, side, -M).astype(F32) + 0.5
        return tuple(reduce_short(xa, first, jnp.where(e < 2, rc, cc), scale, flux))

    short = lax.fori_loop(0, 4, edge_adjoint, tuple(short))
    settle_corner(jnp.int32(3))
    settle_tile(4, short)

    for n in range(9):
        found = out[n]
        rows = [found[:, r * tiles : (r + 1) * tiles] for r in range(cap)]
        if cap < 16:
            rows.append(jnp.zeros((128 - 8 * cap, tiles), F32))
        leaving[pl.ds(n, tiles, stride=9), :] = jnp.concatenate(rows, axis=0).T


def render_and_adjoin(arrived, sky_level, counts, cap):
    _, side, _ = counts.shape
    slots = arrived.shape[0] // 9 * cap
    M, B = MARGIN, BANDS
    chunks = side // M
    vm = lambda *s: pltpu.VMEM(s, BF16)
    vf = lambda *s: pltpu.VMEM(s, F32)
    scratch = [
        vf(9, 8, slots), vf(9, 8, slots), pltpu.VMEM(counts.shape, counts.dtype), vf(chunks, B * M, side),
        vm(chunks + 2, B * M, side), vm(B * M, side), vm(2, B * M, side), vf(2, side, B * M),
        vm(chunks, B * M, slots), vm(side, slots),
        vm(4, B * M, slots), vm(4, side, slots),
        vm(4, B * M, slots), vm(4, M, slots),
        vf(B * M, slots), vf(B * M, slots), vf(side, slots), vf(M, slots),
        pltpu.SemaphoreType.DMA,
    ]
    return pl.pallas_call(
        functools.partial(core, side, cap),
        out_shape=jax.ShapeDtypeStruct(arrived.shape, F32),
        in_specs=[
            pl.BlockSpec(memory_space=pltpu.VMEM),
            pl.BlockSpec(memory_space=pltpu.SMEM),
            pl.BlockSpec(memory_space=pl.ANY),
        ],
        out_specs=pl.BlockSpec(memory_space=pltpu.VMEM),
        scratch_shapes=scratch,
        compiler_params=pltpu.CompilerParams(vmem_limit_bytes=60 * 1024 * 1024),
    )(arrived, sky_level, counts)


def exact_dot(hot, values, contract):
    high = values.astype(BF16)
    rest = values - high.astype(F32)
    middle = rest.astype(BF16)
    low = (rest - middle.astype(F32)).astype(BF16)
    total = None
    for part in (low, middle, high):
        found = lax.dot_general(hot, part, (contract, ((), ())), preferred_element_type=F32)
        total = found if total is None else total + found
    return total


def ranks(owner_row):
    here = owner_row.shape[1]
    first = lax.broadcasted_iota(jnp.int32, (here, here), 0)
    second = lax.broadcasted_iota(jnp.int32, (here, here), 1)
    numbers = owner_row.astype(F32)
    column = jnp.broadcast_to(numbers, (8, here)).T[:, :1]
    same = (column == numbers) & (first < second)
    return jnp.sum(jnp.where(same, 1.0, 0.0), axis=0, keepdims=True).astype(jnp.int32)


def turned(x, shift):
    shift = shift % x.shape[0]
    return x if shift == 0 else jnp.concatenate([x[shift:], x[:shift]], axis=0)


def send_rows(n_ra, n_dec, cap, log_flux, position, log_width, owner, out):
    tiles = n_ra * n_dec
    here = owner.shape[1]
    owner_row = owner[...]
    rank_row = ranks(owner_row)
    rows = jnp.concatenate([log_flux[...], position[...], log_width[...]], axis=0)
    place = lax.broadcasted_iota(jnp.int32, (128, here), 0)
    mine = (place // 8 == rank_row) & (rank_row < cap)
    spread = jnp.where(mine, jnp.concatenate([rows] * 16, axis=0), 0.0)
    hot = (lax.broadcasted_iota(jnp.int32, (tiles, here), 0) == owner_row).astype(F32).astype(BF16)
    contract = ((1,), (1,))
    base = exact_dot(hot, spread, contract)
    taken = lax.dot_general(hot, mine.astype(F32).astype(BF16), (contract, ((), ())), preferred_element_type=F32)
    lane = lax.broadcasted_iota(jnp.int32, (tiles, 128), 1) % 8
    empty = jnp.where(lane < BANDS, EMPTY, 0.0)
    base = jnp.where(taken > 0.5, base, empty)
    tile = lax.broadcasted_iota(jnp.int32, (tiles, 1), 0)
    at_ra, at_dec = tile // n_dec, tile % n_dec
    for n, (i, j) in enumerate(AROUND):
        inside = (at_ra + i >= 0) & (at_ra + i < n_ra) & (at_dec + j >= 0) & (at_dec + j < n_dec)
        out[pl.ds(n, tiles, stride=9), :] = jnp.where(inside, turned(base, i * n_dec + j), empty)


def collect_rows(n_ra, n_dec, cap, arrived, owner, out):
    tiles = n_ra * n_dec
    here = owner.shape[1]
    owner_row = owner[...]
    rank_row = ranks(owner_row)
    total = None
    for n, (i, j) in enumerate(AROUND):
        part = turned(arrived[pl.ds(n, tiles, stride=9), :], -(i * n_dec + j))
        total = part if total is None else total + part
    hot = (lax.broadcasted_iota(jnp.int32, (tiles, here), 0) == owner_row).astype(F32).astype(BF16)
    picked = exact_dot(hot, total, ((0,), (0,))).T
    place = lax.broadcasted_iota(jnp.int32, (128, here), 0) // 8
    picked = jnp.where(place == rank_row, picked, 0.0)
    found = picked[:8]
    for r in range(1, cap):
        found = found + picked[8 * r : 8 * r + 8]
    out[...] = found


def on_device(log_flux, position, log_width, owner_tile, sky_level, counts):
    n_ra, n_dec = lax.axis_size("ra"), lax.axis_size("dec")
    tiles = n_ra * n_dec
    cap = max(2, 2 * CAT_DEV // tiles)
    here = log_flux.shape[1]
    owner = owner_tile.reshape(1, here)
    box = jax.ShapeDtypeStruct((9 * tiles, 128), F32)
    leaving = pl.pallas_call(functools.partial(send_rows, n_ra, n_dec, cap), out_shape=box)(
        log_flux, position, log_width[None, :], owner
    )
    arrived = lax.all_to_all(leaving.reshape(-1), AXES, split_axis=0, concat_axis=0, tiled=True)
    partial = render_and_adjoin(arrived.reshape(box.shape), sky_level, counts, cap)
    back = lax.all_to_all(partial.reshape(-1), AXES, split_axis=0, concat_axis=0, tiled=True)
    return pl.pallas_call(
        functools.partial(collect_rows, n_ra, n_dec, cap), out_shape=jax.ShapeDtypeStruct((8, here), F32)
    )(back.reshape(box.shape), owner)


def solution(mesh):
    in_specs = (
        P(None, AXES),
        P(None, AXES),
        P(AXES),
        P(AXES, None),
        P("ra", "dec", None),
        P(None, "ra", "dec"),
    )
    return jax.shard_map(
        on_device, mesh=mesh, in_specs=in_specs, out_specs=P(None, AXES), check_vma=False
    )
```

time: 75.5 us -> 61.1 us (0.81)
  local copies, waits for them, and re-layouts: 6.8 us -> 0 us
  other arithmetic: 2.39 us -> 0 us
  matrix products: 2.07 us -> 0 us
  blocking collectives: 30 us -> 28 us
  Pallas kernels: 33.7 us -> 32.8 us
    reshape x10 -> x0, local copies, waits for them, and re-layouts: 4.54 us -> none  [the longest x2 1.66 us: on_device(): grads.reshape(9, 8, tiles, cap).transpose(2, 1, 0, 3)]
    dot_general x2 -> x0, matrix products: 2.07 us -> none  [the longest x1 1.06 us: on_device(): sorted_rows = jnp.dot(rows, onehot, precision=lax.Precision.HIGHEST)]
    all_to_all x2, blocking collectives: 30 us -> 28 us  [the longest x1 16 us: on_device(): lax.all_to_all(leaving.reshape(-1), AXES, split_axis=0, concat_axis=0, ti...]
    transpose x4 -> x0, local copies, waits for them, and re-layouts: 1.53 us -> none  [the longest x1 0.74 us: on_device(): outgoing = outgoing.transpose(2, 3, 1, 0, 4).reshape(tiles, 8, 9 * cap)]
    add x2 -> x0, other arithmetic: 1.32 us -> none  [the longest x1 0.69 us: on_device(): slot = target * cap + rank]
    reduce_sum x1 -> x0, other arithmetic: 0.93 us -> none  [on_device(): rank = jnp.sum(matches.astype(jnp.int32), axis=1)]
    pallas_call x1 -> x3, Pallas kernels: 33.7 us -> 32.8 us  [the longest x1 29.1 us: render_and_adjoin(): pl.pallas_call(functools.partial(core, side, cap), out_shape=jax.ShapeDty...]
where the time goes in v3:
time: 61.1 us; the launch traced here: 60.8 us
  Pallas kernels  32.8 us (54%)
  blocking collectives  28 us (46%)
    pallas_call x1, Pallas kernels, render_and_adjoin(): pl.pallas_call(functools.partial(core, side, cap), out_shape=jax.ShapeDty...  29.1 us
    all_to_all x1, blocking collectives, on_device(): lax.all_to_all(leaving.reshape(-1), AXES, split_axis=0, concat_axis=0, ti...  16 us
    all_to_all x1, blocking collectives, on_device(): lax.all_to_all(partial.reshape(-1), AXES, split_axis=0, concat_axis=0, ti...  11.9 us
    pallas_call x1, Pallas kernels, on_device(): pl.pallas_call(functools.partial(collect_rows, n_ra, n_dec, cap), out_sha...  1.86 us
    pallas_call x1, Pallas kernels, on_device(): pl.pallas_call(functools.partial(send_rows, n_ra, n_dec, cap), out_shape=...  1.86 us

profile of v3, /device:TPU:0, one launch (start us, length us, event | category | flops | bytes accessed | tf_op | source)
XLA Modules:
  0.0 60.8 jit_solution(11210974451804242964)
XLA Ops:
  0.0 1.9 %shard_map.64 = f32[288,128]{1,0:T(8,128)} custom-call(f32[5,256]{1,0:T(8,128)} %log_flux.1, f32[2,256]{1,0:T(2,128)} %position.1, f32[1,256]{1,0:T(1,128)} %bitcast.12, s32[1,256]{1,0:T(1,128)} %bitcast.10), custom_call_target="tpu_custom_call" | custom-call | tf_op jit(solution)/shard_map/pallas_call | solution.py:370
  1.9 16.0 %all_to_all.18 = f32[32,1152,1]{1,2,0:T(1,128)} all-to-all(f32[32,1152,1]{1,2,0:T(1,128)} %bitcast.7), channel_id=1, replica_groups=mesh['ra'=8,'dec'=4] {'ra','dec'}, dimensions={0} | all-to-all | bytes 294912 | tf_op jit(solution)/shard_map/all_to_all | solution.py:373
  17.9 29.1 %shard_map.65 = f32[288,128]{1,0:T(8,128)} custom-call(f32[288,128]{1,0:T(8,128)} %bitcast.8, f32[1,1,5]{2,1,0:T(1,128)} %sky.1, s32[5,640,640]{2,1,0:T(8,128)} %counts_hbm.1), custom_call_target="tpu_custom_call" | custom-call | tf_op jit(solution)/shard_map/pallas_call | solution.py:280
  47.0 11.9 %all_to_all.19 = f32[32,1152,1]{1,2,0:T(1,128)} all-to-all(f32[32,1152,1]{1,2,0:T(1,128)} %bitcast.9), channel_id=1, replica_groups=mesh['ra'=8,'dec'=4] {'ra','dec'}, dimensions={0} | all-to-all | bytes 294912 | tf_op jit(solution)/shard_map/all_to_all | solution.py:375
  58.9 1.9 %shard_map.66 = f32[8,256]{1,0:T(8,128)} custom-call(f32[288,128]{1,0:T(8,128)} %bitcast.6, s32[1,256]{1,0:T(1,128)} %bitcast.11), custom_call_target="tpu_custom_call" | custom-call | tf_op jit(solution)/shard_map/pallas_call | solution.py:376

commit v4 on v3

v4 whole, which is shorter than its diff:
```python
import functools
import math

import jax
import jax.numpy as jnp
from jax import lax
from jax.experimental import pallas as pl
from jax.experimental.pallas import tpu as pltpu
from jax.sharding import PartitionSpec as P

MARGIN = 128
CAT_DEV = 256
BANDS = 5
AXES = ("ra", "dec")
AROUND = [(0, 0), (-1, 0), (1, 0), (0, -1), (0, 1), (-1, -1), (-1, 1), (1, -1), (1, 1)]
EMPTY = -1e30
F32 = jnp.float32
BF16 = jnp.bfloat16


def dot(a, b):
    return jnp.dot(a, b, preferred_element_type=F32)


def dot_nt(a, b):
    return lax.dot_general(a, b, (((1,), (1,)), ((), ())), preferred_element_type=F32)


def dot_tn(a, b):
    return lax.dot_general(a, b, (((0,), (0,)), ((), ())), preferred_element_type=F32)


ROW, COL, INVERSE, SCALE, PEAK, PEAKS = 5, 6, 7, 8, 9, 16


def derive(table, rows):
    index = lax.broadcasted_iota(jnp.int32, rows.shape, 0)
    powers = jnp.exp(jnp.where(index < BANDS, rows, jnp.where(index == 7, -rows, 0.0)))
    inverse = powers[7:8] * (1.0 / MARGIN)
    peak = inverse * (1.0 / math.sqrt(2.0 * math.pi))
    table[:7] = jnp.where(index < BANDS, powers, rows)[:7]
    table[INVERSE : INVERSE + 1] = inverse
    table[SCALE : SCALE + 1] = inverse * inverse * (-0.5 * math.log2(math.e))
    table[PEAK : PEAK + 1] = peak
    table[PEAKS : PEAKS + 8] = powers * peak


def row(table, i, lanes=slice(None)):
    if isinstance(i, int):
        return table[i : i + 1, lanes]
    return jnp.where(i == ROW, table[ROW : ROW + 1, lanes], table[COL : COL + 1, lanes])


def distance(first, count, center):
    return lax.broadcasted_iota(jnp.int32, (count, 1), 0).astype(F32) + first - center


def fill_long(ref, full, length, first, table, axis, step=32, width=128):
    for lo in range(0, ref.shape[1], width):
        lanes = slice(lo, lo + width)
        d0 = distance(first, step, row(table, axis, lanes))
        scale, peak = row(table, SCALE, lanes), row(table, PEAK, lanes)
        for r in range(0, length, step):
            d = d0 + float(r)
            p = jnp.exp2(d * (d * scale)) * peak
            full[r : r + step, lanes] = p
            ref[r : r + step, lanes] = p.astype(BF16)


def fill_scaled(ref, first, table, axis, step=32, width=128):
    for lo in range(0, ref.shape[1], width):
        lanes = slice(lo, lo + width)
        d0 = distance(first, step, row(table, axis, lanes))
        scale = row(table, SCALE, lanes)
        peaks = [row(table, PEAKS + b, lanes) for b in range(BANDS)]
        for r in range(0, MARGIN, step):
            d = d0 + float(r)
            e = jnp.exp2(d * (d * scale))
            for b in range(BANDS):
                ref[b * MARGIN + r : b * MARGIN + r + step, lanes] = (e * peaks[b]).astype(BF16)


def fold(x):
    total = x[:8]
    for i in range(8, x.shape[0], 8):
        total = total + x[i : i + 8]
    return total


def reduce_short(buf, first, table, axis, step=32, width=128):
    parts = []
    for lo in range(0, buf.shape[1], width):
        lanes = slice(lo, lo + width)
        fluxes = [row(table, b, lanes) for b in range(BANDS)]
        scale = row(table, SCALE, lanes)
        d0 = distance(first, step, row(table, axis, lanes))
        sums = None
        for r in range(0, MARGIN, step):
            d = d0 + float(r)
            e = jnp.exp2(d * (d * scale))
            new = []
            total = None
            for b in range(BANDS):
                a = buf[b * MARGIN + r : b * MARGIN + r + step, lanes] * e
                new.append(fold(a))
                a = a * fluxes[b]
                total = a if total is None else total + a
            q = total * d
            new.extend([fold(q), fold(q * d)])
            sums = new if sums is None else [s + v for s, v in zip(sums, new)]
        parts.append([s * f for s, f in zip(sums, fluxes)] + sums[BANDS:])
    return [jnp.concatenate([p[m] for p in parts], axis=1) for m in range(BANDS + 2)]


def reduce_long(buf, shape, length, first, table, axis, step=32, width=128):
    parts = []
    for lo in range(0, buf.shape[1], width):
        lanes = slice(lo, lo + width)
        d0 = distance(first, step, row(table, axis, lanes))
        sums = None
        for r in range(0, length, step):
            q = shape[r : r + step, lanes] * buf[r : r + step, lanes]
            d = d0 + float(r)
            q1 = q * d
            new = [fold(q), fold(q1), fold(q1 * d)]
            sums = new if sums is None else [s + v for s, v in zip(sums, new)]
        parts.append(sums)
    return [jnp.concatenate([p[m] for p in parts], axis=1) for m in range(3)]


def settle(short, long, table):
    peak, inverse = row(table, PEAK), row(table, INVERSE)
    short = [jnp.sum(v, axis=0, keepdims=True) * peak for v in short]
    long = [jnp.sum(v, axis=0, keepdims=True) for v in long]
    square = inverse * inverse
    bands = short[:BANDS]
    zeroth = bands[0] + bands[1] + bands[2] + bands[3] + bands[4]
    width = square * short[BANDS + 1] - zeroth + (square * long[2] - long[0])
    return bands, square * short[BANDS], square * long[1], width


def core(side, cap, arrived, sky, counts_hbm, leaving, prm, out, counts, canvas, w, rim_sum,
         c_sc, e_sc, e_long, k_sc, k_long, xa, xb, yb, yk, e_full, k_full, sem):
    M = MARGIN
    chunks = side // M
    last = side - M
    fetch = pltpu.make_async_copy(counts_hbm, counts, sem)
    fetch.start()
    tiles = arrived.shape[0] // 9
    slots = prm.shape[2]
    for n in range(9):
        table = arrived[pl.ds(n, tiles, stride=9), :].T
        derive(prm.at[n], jnp.concatenate([table[8 * r : 8 * r + 8] for r in range(cap)], axis=1))

    def number(c):
        return c.astype(F32) * float(M) + 0.5

    def rim_at(i):
        return side if i % 2 == 0 else -M

    own = prm.at[0]

    def own_fill(c, _):
        at = pl.multiple_of(c * M, M)
        fill_long(e_long.at[0, pl.ds(at, M), :], e_full.at[0, pl.ds(at, M), :], M, number(c), own, COL)
        fill_scaled(c_sc.at[c], number(c), own, ROW)
        return 0

    lax.fori_loop(0, chunks, own_fill, 0)

    for c in range(chunks):
        canvas[c] = dot_nt(c_sc[c], e_long[0])
        if c < 4:
            across, along = (ROW, COL) if c < 2 else (COL, ROW)
            fill_scaled(e_sc.at[c], (side if c % 2 == 0 else -M) + 0.5, prm.at[1 + c], across)
            fill_long(e_long.at[1 + c], e_full.at[1 + c], side, 0.5, prm.at[1 + c], along)
            fill_scaled(k_sc.at[c], (side if c % 2 == 0 else -M) + 0.5, prm.at[5 + c], COL)
            fill_long(k_long.at[c], k_full.at[c], M, (side if c < 2 else -M) + 0.5, prm.at[5 + c], ROW)

    def rim_render(v, _):
        rim_sum[v] = dot_nt(e_long[3 + v], e_sc[2 + v])
        canvas[v * (chunks - 1)] += dot_nt(e_sc[v], e_long[1 + v])
        rim_sum[v, :M] += dot_nt(k_long[v], k_sc[v])
        rim_sum[v, last:] += dot_nt(k_long[2 + v], k_sc[2 + v])
        return 0

    for v in range(2):
        rim_render(v, 0)

    fetch.wait()

    def weigh(c, own):
        rows = slice(c * M, c * M + M)
        for b in range(BANDS):
            band = slice(b * M, (b + 1) * M)
            level = sky[0, 0, b]
            seen = counts[b, rows, :].astype(F32)
            left = canvas[c, band, :M] + rim_sum[0, rows, band]
            right = canvas[c, band, last:] + rim_sum[1, rows, band]
            model = jnp.concatenate([left, canvas[c, band, M:last], right], axis=1)
            weights = (seen / (model + level) - 1.0).astype(BF16)
            own[band, :] = weights
            w[chunks, band, rows] = weights[:, :M].T
            w[chunks + 1, band, rows] = weights[:, last:].T

    weigh(0, w.at[0])

    own_short = None
    for c in range(chunks):
        if c > 0:
            found = reduce_short(xa, (c - 1) * M + 0.5, own, ROW)
            own_short = found if own_short is None else [s + f for s, f in zip(own_short, found)]
        xa[...] = dot(w[c], e_long[0])
        part = dot_tn(w[c], c_sc[c])
        yb[...] = part if c == 0 else yb[...] + part
        if c < chunks - 1:
            weigh(c + 1, w.at[c + 1])

    def settle_tile(g):
        table = prm.at[g]
        short_axis, long_axis = (ROW, COL) if g < 3 else (COL, ROW)
        first = (last if g == 0 else rim_at(g - 1)) + 0.5
        short = reduce_short(xa, first, table, short_axis)
        if g == 0:
            short = [s + h for s, h in zip(short, own_short)]
        long = reduce_long(yb, e_full.at[g], side, 0.5, table, long_axis)
        bands, across, along, width = settle(short, long, table)
        grads = [across, along] if g < 3 else [along, across]
        out[g] = jnp.concatenate(bands + grads + [width], axis=0)

    def settle_corner(k):
        table = prm.at[5 + k]
        found = reduce_short(xb, rim_at(k) + 0.5, table, COL)
        long = reduce_long(yk, k_full.at[k], M, rim_at(k // 2) + 0.5, table, ROW)
        bands, col_grad, row_grad, width = settle(found, long, table)
        out[5 + k] = jnp.concatenate(bands + [row_grad, col_grad, width], axis=0)

    for e in range(4):
        settle_tile(e)
        if e > 0:
            settle_corner(e - 1)
        strip = (0, chunks - 1, chunks, chunks + 1)[e]
        rim, at = chunks + e % 2, slice(e // 2 * last, e // 2 * last + M)
        xa[...] = dot(w[strip], e_long[1 + e])
        xb[...] = dot(w[rim, :, at], k_long[e])
        yk[...] = dot_tn(w[rim, :, at], k_sc[e])
        yb[...] = dot_tn(w[strip], e_sc[e])
    settle_corner(3)
    settle_tile(4)

    for n in range(9):
        found = out[n]
        rows = [found[:, r * tiles : (r + 1) * tiles] for r in range(cap)]
        if cap < 16:
            rows.append(jnp.zeros((128 - 8 * cap, tiles), F32))
        leaving[pl.ds(n, tiles, stride=9), :] = jnp.concatenate(rows, axis=0).T


def render_and_adjoin(arrived, sky_level, counts, cap):
    _, side, _ = counts.shape
    slots = arrived.shape[0] // 9 * cap
    M, B = MARGIN, BANDS
    chunks = side // M
    vm = lambda *s: pltpu.VMEM(s, BF16)
    vf = lambda *s: pltpu.VMEM(s, F32)
    scratch = [
        vf(9, 24, slots), vf(9, 8, slots), pltpu.VMEM(counts.shape, counts.dtype), vf(chunks, B * M, side),
        vm(chunks + 2, B * M, side), vf(2, side, B * M),
        vm(chunks, B * M, slots),
        vm(4, B * M, slots), vm(5, side, slots),
        vm(4, B * M, slots), vm(4, M, slots),
        vf(B * M, slots), vf(B * M, slots), vf(side, slots), vf(M, slots),
        vf(5, side, slots), vf(4, M, slots),
        pltpu.SemaphoreType.DMA,
    ]
    return pl.pallas_call(
        functools.partial(core, side, cap),
        out_shape=jax.ShapeDtypeStruct(arrived.shape, F32),
        in_specs=[
            pl.BlockSpec(memory_space=pltpu.VMEM),
            pl.BlockSpec(memory_space=pltpu.SMEM),
            pl.BlockSpec(memory_space=pl.ANY),
        ],
        out_specs=pl.BlockSpec(memory_space=pltpu.VMEM),
        scratch_shapes=scratch,
        compiler_params=pltpu.CompilerParams(vmem_limit_bytes=60 * 1024 * 1024),
    )(arrived, sky_level, counts)


def exact_dot(hot, values, contract):
    high = values.astype(BF16)
    rest = values - high.astype(F32)
    middle = rest.astype(BF16)
    low = (rest - middle.astype(F32)).astype(BF16)
    total = None
    for part in (low, middle, high):
        found = lax.dot_general(hot, part, (contract, ((), ())), preferred_element_type=F32)
        total = found if total is None else total + found
    return total


def ranks(owner_row):
    here = owner_row.shape[1]
    first = lax.broadcasted_iota(jnp.int32, (here, here), 0)
    second = lax.broadcasted_iota(jnp.int32, (here, here), 1)
    numbers = owner_row.astype(F32)
    column = jnp.broadcast_to(numbers, (8, here)).T[:, :1]
    same = (column == numbers) & (first < second)
    return jnp.sum(jnp.where(same, 1.0, 0.0), axis=0, keepdims=True).astype(jnp.int32)


def turned(x, shift):
    shift = shift % x.shape[0]
    return x if shift == 0 else jnp.concatenate([x[shift:], x[:shift]], axis=0)


def send_rows(n_ra, n_dec, cap, log_flux, position, log_width, owner, out):
    tiles = n_ra * n_dec
    here = owner.shape[1]
    owner_row = owner[...]
    rank_row = ranks(owner_row)
    rows = jnp.concatenate([log_flux[...], position[...], log_width[...]], axis=0)
    place = lax.broadcasted_iota(jnp.int32, (128, here), 0)
    mine = (place // 8 == rank_row) & (rank_row < cap)
    spread = jnp.where(mine, jnp.concatenate([rows] * 16, axis=0), 0.0)
    hot = (lax.broadcasted_iota(jnp.int32, (tiles, here), 0) == owner_row).astype(F32).astype(BF16)
    contract = ((1,), (1,))
    base = exact_dot(hot, spread, contract)
    taken = lax.dot_general(hot, mine.astype(F32).astype(BF16), (contract, ((), ())), preferred_element_type=F32)
    lane = lax.broadcasted_iota(jnp.int32, (tiles, 128), 1) % 8
    empty = jnp.where(lane < BANDS, EMPTY, 0.0)
    base = jnp.where(taken > 0.5, base, empty)
    tile = lax.broadcasted_iota(jnp.int32, (tiles, 1), 0)
    at_ra, at_dec = tile // n_dec, tile % n_dec
    for n, (i, j) in enumerate(AROUND):
        inside = (at_ra + i >= 0) & (at_ra + i < n_ra) & (at_dec + j >= 0) & (at_dec + j < n_dec)
        out[pl.ds(n, tiles, stride=9), :] = jnp.where(inside, turned(base, i * n_dec + j), empty)


def collect_rows(n_ra, n_dec, cap, arrived, owner, out):
    tiles = n_ra * n_dec
    here = owner.shape[1]
    owner_row = owner[...]
    rank_row = ranks(owner_row)
    total = None
    for n, (i, j) in enumerate(AROUND):
        part = turned(arrived[pl.ds(n, tiles, stride=9), :], -(i * n_dec + j))
        total = part if total is None else total + part
    hot = (lax.broadcasted_iota(jnp.int32, (tiles, here), 0) == owner_row).astype(F32).astype(BF16)
    picked = exact_dot(hot, total, ((0,), (0,))).T
    place = lax.broadcasted_iota(jnp.int32, (128, here), 0) // 8
    picked = jnp.where(place == rank_row, picked, 0.0)
    found = picked[:8]
    for r in range(1, cap):
        found = found + picked[8 * r : 8 * r + 8]
    out[...] = found


def on_device(log_flux, position, log_width, owner_tile, sky_level, counts):
    n_ra, n_dec = lax.axis_size("ra"), lax.axis_size("dec")
    tiles = n_ra * n_dec
    cap = max(2, 2 * CAT_DEV // tiles)
    here = log_flux.shape[1]
    owner = owner_tile.reshape(1, here)
    box = jax.ShapeDtypeStruct((9 * tiles, 128), F32)
    leaving = pl.pallas_call(functools.partial(send_rows, n_ra, n_dec, cap), out_shape=box)(
        log_flux, position, log_width[None, :], owner
    )
    arrived = lax.all_to_all(leaving.reshape(-1), AXES, split_axis=0, concat_axis=0, tiled=True)
    partial = render_and_adjoin(arrived.reshape(box.shape), sky_level, counts, cap)
    back = lax.all_to_all(partial.reshape(-1), AXES, split_axis=0, concat_axis=0, tiled=True)
    return pl.pallas_call(
        functools.partial(collect_rows, n_ra, n_dec, cap), out_shape=jax.ShapeDtypeStruct((8, here), F32)
    )(back.reshape(box.shape), owner)


def solution(mesh):
    in_specs = (
        P(None, AXES),
        P(None, AXES),
        P(AXES),
        P(AXES, None),
        P("ra", "dec", None),
        P(None, "ra", "dec"),
    )
    return jax.shard_map(
        on_device, mesh=mesh, in_specs=in_specs, out_specs=P(None, AXES), check_vma=False
    )
```

time: 61.1 us -> 54.4 us (0.89)
  Pallas kernels: 32.8 us -> 26.1 us
    pallas_call x1, Pallas kernels: 29.1 us -> 22.4 us  [render_and_adjoin(): pl.pallas_call(functools.partial(core, side, cap), out_shape=jax.ShapeDty...]
where the time goes in v4:
time: 54.4 us; the launch traced here: 54.1 us
  blocking collectives  28 us (51%)
  Pallas kernels  26.1 us (48%)
    pallas_call x1, Pallas kernels, render_and_adjoin(): pl.pallas_call(functools.partial(core, side, cap), out_shape=jax.ShapeDty...  22.4 us
    all_to_all x1, blocking collectives, on_device(): lax.all_to_all(leaving.reshape(-1), AXES, split_axis=0, concat_axis=0, ti...  16 us
    all_to_all x1, blocking collectives, on_device(): lax.all_to_all(partial.reshape(-1), AXES, split_axis=0, concat_axis=0, ti...  11.9 us
    pallas_call x1, Pallas kernels, on_device(): pl.pallas_call(functools.partial(collect_rows, n_ra, n_dec, cap), out_sha...  1.86 us
    pallas_call x1, Pallas kernels, on_device(): pl.pallas_call(functools.partial(send_rows, n_ra, n_dec, cap), out_shape=...  1.86 us

profile of v4, /device:TPU:0, one launch (start us, length us, event | category | flops | bytes accessed | tf_op | source)
XLA Modules:
  0.0 54.1 jit_solution(6679140366901984332)
XLA Ops:
  0.0 1.9 %shard_map.64 = f32[288,128]{1,0:T(8,128)} custom-call(f32[5,256]{1,0:T(8,128)} %log_flux.1, f32[2,256]{1,0:T(2,128)} %position.1, f32[1,256]{1,0:T(1,128)} %bitcast.12, s32[1,256]{1,0:T(1,128)} %bitcast.10), custom_call_target="tpu_custom_call" | custom-call | tf_op jit(solution)/shard_map/pallas_call | solution.py:366
  1.9 16.0 %all_to_all.18 = f32[32,1152,1]{1,2,0:T(1,128)} all-to-all(f32[32,1152,1]{1,2,0:T(1,128)} %bitcast.7), channel_id=1, replica_groups=mesh['ra'=8,'dec'=4] {'ra','dec'}, dimensions={0} | all-to-all | bytes 294912 | tf_op jit(solution)/shard_map/all_to_all | solution.py:369
  17.9 22.4 %shard_map.65 = f32[288,128]{1,0:T(8,128)} custom-call(f32[288,128]{1,0:T(8,128)} %bitcast.8, f32[1,1,5]{2,1,0:T(1,128)} %sky.1, s32[5,640,640]{2,1,0:T(8,128)} %counts_hbm.1), custom_call_target="tpu_custom_call" | custom-call | tf_op jit(solution)/shard_map/pallas_call | solution.py:276
  40.3 11.9 %all_to_all.19 = f32[32,1152,1]{1,2,0:T(1,128)} all-to-all(f32[32,1152,1]{1,2,0:T(1,128)} %bitcast.9), channel_id=1, replica_groups=mesh['ra'=8,'dec'=4] {'ra','dec'}, dimensions={0} | all-to-all | bytes 294912 | tf_op jit(solution)/shard_map/all_to_all | solution.py:371
  52.2 1.9 %shard_map.66 = f32[8,256]{1,0:T(8,128)} custom-call(f32[288,128]{1,0:T(8,128)} %bitcast.6, s32[1,256]{1,0:T(1,128)} %bitcast.11), custom_call_target="tpu_custom_call" | custom-call | tf_op jit(solution)/shard_map/pallas_call | solution.py:372

commit v5 on v4

--- a/solution.py
+++ b/solution.py
@@ -160,22 +160,19 @@
 
     own = prm.at[0]
 
-    def own_fill(c, _):
-        at = pl.multiple_of(c * M, M)
-        fill_long(e_long.at[0, pl.ds(at, M), :], e_full.at[0, pl.ds(at, M), :], M, number(c), own, COL)
-        fill_scaled(c_sc.at[c], number(c), own, ROW)
-        return 0
-
-    lax.fori_loop(0, chunks, own_fill, 0)
-
     for c in range(chunks):
+        rows = pl.ds(c * M, M)
+        fill_long(e_long.at[0, rows, :], e_full.at[0, rows, :], M, c * M + 0.5, own, COL)
+
+    for c in range(chunks):
+        fill_scaled(c_sc.at[c], c * M + 0.5, own, ROW)
         canvas[c] = dot_nt(c_sc[c], e_long[0])
         if c < 4:
             across, along = (ROW, COL) if c < 2 else (COL, ROW)
-            fill_scaled(e_sc.at[c], (side if c % 2 == 0 else -M) + 0.5, prm.at[1 + c], across)
+            fill_scaled(e_sc.at[c], rim_at(c) + 0.5, prm.at[1 + c], across)
             fill_long(e_long.at[1 + c], e_full.at[1 + c], side, 0.5, prm.at[1 + c], along)
-            fill_scaled(k_sc.at[c], (side if c % 2 == 0 else -M) + 0.5, prm.at[5 + c], COL)
-            fill_long(k_long.at[c], k_full.at[c], M, (side if c < 2 else -M) + 0.5, prm.at[5 + c], ROW)
+            fill_scaled(k_sc.at[c], rim_at(c) + 0.5, prm.at[5 + c], COL)
+            fill_long(k_long.at[c], k_full.at[c], M, rim_at(c // 2) + 0.5, prm.at[5 + c], ROW)
 
     def rim_render(v, _):
         rim_sum[v] = dot_nt(e_long[3 + v], e_sc[2 + v])
@@ -211,10 +208,10 @@
             found = reduce_short(xa, (c - 1) * M + 0.5, own, ROW)
             own_short = found if own_short is None else [s + f for s, f in zip(own_short, found)]
         xa[...] = dot(w[c], e_long[0])
-        part = dot_tn(w[c], c_sc[c])
-        yb[...] = part if c == 0 else yb[...] + part
         if c < chunks - 1:
             weigh(c + 1, w.at[c + 1])
+    both = lambda ref: ref[:chunks].reshape(chunks * BANDS * M, -1)
+    yb[...] = dot_tn(both(w), both(c_sc))
 
     def settle_tile(g):
         table = prm.at[g]

time: 54.4 us -> 53.3 us (0.980)
  Pallas kernels: 26.1 us -> 25 us
    pallas_call x1, Pallas kernels: 22.4 us -> 21.3 us  [render_and_adjoin(): pl.pallas_call(functools.partial(core, side, cap), out_shape=jax.ShapeDty...]
where the time goes in v5:
time: 53.3 us; the launch traced here: 53 us
  blocking collectives  28 us (53%)
  Pallas kernels  25 us (47%)
    pallas_call x1, Pallas kernels, render_and_adjoin(): pl.pallas_call(functools.partial(core, side, cap), out_shape=jax.ShapeDty...  21.3 us
    all_to_all x1, blocking collectives, on_device(): lax.all_to_all(leaving.reshape(-1), AXES, split_axis=0, concat_axis=0, ti...  16 us
    all_to_all x1, blocking collectives, on_device(): lax.all_to_all(partial.reshape(-1), AXES, split_axis=0, concat_axis=0, ti...  11.9 us
    pallas_call x1, Pallas kernels, on_device(): pl.pallas_call(functools.partial(collect_rows, n_ra, n_dec, cap), out_sha...  1.86 us
    pallas_call x1, Pallas kernels, on_device(): pl.pallas_call(functools.partial(send_rows, n_ra, n_dec, cap), out_shape=...  1.86 us

profile of v5, /device:TPU:0, one launch (start us, length us, event | category | flops | bytes accessed | tf_op | source)
XLA Modules:
  0.0 53.0 jit_solution(1557213819732240937)
XLA Ops:
  0.0 1.9 %shard_map.64 = f32[288,128]{1,0:T(8,128)} custom-call(f32[5,256]{1,0:T(8,128)} %log_flux.1, f32[2,256]{1,0:T(2,128)} %position.1, f32[1,256]{1,0:T(1,128)} %bitcast.12, s32[1,256]{1,0:T(1,128)} %bitcast.10), custom_call_target="tpu_custom_call" | custom-call | tf_op jit(solution)/shard_map/pallas_call | solution.py:363
  1.9 16.0 %all_to_all.18 = f32[32,1152,1]{1,2,0:T(1,128)} all-to-all(f32[32,1152,1]{1,2,0:T(1,128)} %bitcast.7), channel_id=1, replica_groups=mesh['ra'=8,'dec'=4] {'ra','dec'}, dimensions={0} | all-to-all | bytes 294912 | tf_op jit(solution)/shard_map/all_to_all | solution.py:366
  17.9 21.3 %shard_map.65 = f32[288,128]{1,0:T(8,128)} custom-call(f32[288,128]{1,0:T(8,128)} %bitcast.8, f32[1,1,5]{2,1,0:T(1,128)} %sky.1, s32[5,640,640]{2,1,0:T(8,128)} %counts_hbm.1), custom_call_target="tpu_custom_call" | custom-call | tf_op jit(solution)/shard_map/pallas_call | solution.py:273
  39.2 11.9 %all_to_all.19 = f32[32,1152,1]{1,2,0:T(1,128)} all-to-all(f32[32,1152,1]{1,2,0:T(1,128)} %bitcast.9), channel_id=1, replica_groups=mesh['ra'=8,'dec'=4] {'ra','dec'}, dimensions={0} | all-to-all | bytes 294912 | tf_op jit(solution)/shard_map/all_to_all | solution.py:368
  51.1 1.9 %shard_map.66 = f32[8,256]{1,0:T(8,128)} custom-call(f32[288,128]{1,0:T(8,128)} %bitcast.6, s32[1,256]{1,0:T(1,128)} %bitcast.11), custom_call_target="tpu_custom_call" | custom-call | tf_op jit(solution)/shard_map/pallas_call | solution.py:369

commit v6 on v5

--- a/solution.py
+++ b/solution.py
@@ -174,15 +174,12 @@
             fill_scaled(k_sc.at[c], rim_at(c) + 0.5, prm.at[5 + c], COL)
             fill_long(k_long.at[c], k_full.at[c], M, rim_at(c // 2) + 0.5, prm.at[5 + c], ROW)
 
-    def rim_render(v, _):
+    for v in range(2):
         rim_sum[v] = dot_nt(e_long[3 + v], e_sc[2 + v])
+    for v in range(2):
         canvas[v * (chunks - 1)] += dot_nt(e_sc[v], e_long[1 + v])
         rim_sum[v, :M] += dot_nt(k_long[v], k_sc[v])
         rim_sum[v, last:] += dot_nt(k_long[2 + v], k_sc[2 + v])
-        return 0
-
-    for v in range(2):
-        rim_render(v, 0)
 
     fetch.wait()
 
@@ -200,16 +197,17 @@
             w[chunks, band, rows] = weights[:, :M].T
             w[chunks + 1, band, rows] = weights[:, last:].T
 
-    weigh(0, w.at[0])
+    order = list(range(1, chunks - 1)) + [0, chunks - 1]
+    weigh(order[0], w.at[order[0]])
 
     own_short = None
-    for c in range(chunks):
-        if c > 0:
-            found = reduce_short(xa, (c - 1) * M + 0.5, own, ROW)
+    for i, c in enumerate(order):
+        if i > 0:
+            found = reduce_short(xa, order[i - 1] * M + 0.5, own, ROW)
             own_short = found if own_short is None else [s + f for s, f in zip(own_short, found)]
         xa[...] = dot(w[c], e_long[0])
-        if c < chunks - 1:
-            weigh(c + 1, w.at[c + 1])
+        if i < chunks - 1:
+            weigh(order[i + 1], w.at[order[i + 1]])
     both = lambda ref: ref[:chunks].reshape(chunks * BANDS * M, -1)
     yb[...] = dot_tn(both(w), both(c_sc))
 

time: 53.3 us -> 52.7 us (0.989)
  Pallas kernels: 25 us -> 24.4 us
    pallas_call x1, Pallas kernels: 21.3 us -> 20.7 us  [render_and_adjoin(): pl.pallas_call(functools.partial(core, side, cap), out_shape=jax.ShapeDty...]
where the time goes in v6:
time: 52.7 us; the launch traced here: 52.4 us
  blocking collectives  28 us (53%)
  Pallas kernels  24.4 us (46%)
    pallas_call x1, Pallas kernels, render_and_adjoin(): pl.pallas_call(functools.partial(core, side, cap), out_shape=jax.ShapeDty...  20.7 us
    all_to_all x1, blocking collectives, on_device(): lax.all_to_all(leaving.reshape(-1), AXES, split_axis=0, concat_axis=0, ti...  16 us
    all_to_all x1, blocking collectives, on_device(): lax.all_to_all(partial.reshape(-1), AXES, split_axis=0, concat_axis=0, ti...  11.9 us
    pallas_call x1, Pallas kernels, on_device(): pl.pallas_call(functools.partial(collect_rows, n_ra, n_dec, cap), out_sha...  1.86 us
    pallas_call x1, Pallas kernels, on_device(): pl.pallas_call(functools.partial(send_rows, n_ra, n_dec, cap), out_shape=...  1.86 us

profile of v6, /device:TPU:0, one launch (start us, length us, event | category | flops | bytes accessed | tf_op | source)
XLA Modules:
  0.0 52.4 jit_solution(4229903232726896509)
XLA Ops:
  0.0 1.9 %shard_map.64 = f32[288,128]{1,0:T(8,128)} custom-call(f32[5,256]{1,0:T(8,128)} %log_flux.1, f32[2,256]{1,0:T(2,128)} %position.1, f32[1,256]{1,0:T(1,128)} %bitcast.12, s32[1,256]{1,0:T(1,128)} %bitcast.10), custom_call_target="tpu_custom_call" | custom-call | tf_op jit(solution)/shard_map/pallas_call | solution.py:361
  1.9 16.0 %all_to_all.18 = f32[32,1152,1]{1,2,0:T(1,128)} all-to-all(f32[32,1152,1]{1,2,0:T(1,128)} %bitcast.7), channel_id=1, replica_groups=mesh['ra'=8,'dec'=4] {'ra','dec'}, dimensions={0} | all-to-all | bytes 294912 | tf_op jit(solution)/shard_map/all_to_all | solution.py:364
  17.9 20.7 %shard_map.65 = f32[288,128]{1,0:T(8,128)} custom-call(f32[288,128]{1,0:T(8,128)} %bitcast.8, f32[1,1,5]{2,1,0:T(1,128)} %sky.1, s32[5,640,640]{2,1,0:T(8,128)} %counts_hbm.1), custom_call_target="tpu_custom_call" | custom-call | tf_op jit(solution)/shard_map/pallas_call | solution.py:271
  38.6 11.9 %all_to_all.19 = f32[32,1152,1]{1,2,0:T(1,128)} all-to-all(f32[32,1152,1]{1,2,0:T(1,128)} %bitcast.9), channel_id=1, replica_groups=mesh['ra'=8,'dec'=4] {'ra','dec'}, dimensions={0} | all-to-all | bytes 294912 | tf_op jit(solution)/shard_map/all_to_all | solution.py:366
  50.5 1.9 %shard_map.66 = f32[8,256]{1,0:T(8,128)} custom-call(f32[288,128]{1,0:T(8,128)} %bitcast.6, s32[1,256]{1,0:T(1,128)} %bitcast.11), custom_call_target="tpu_custom_call" | custom-call | tf_op jit(solution)/shard_map/pallas_call | solution.py:367
